TPU v7x, 32 devices: a whole 2x2x4 slice. The times are simulated.
32 devices in a mesh: row: 8 (over z, y), col: 2 (over x), layer: 2 (over core).
Axes of the slice: x: 2, y: 2, z: 4, core: 2. Of those that a mesh axis runs over, the one named last changes fastest.
Arguments:
- p_blocks: bfloat16 [128, 10, 128, 128], P('row', 'col'), may hold values from -1.1953125 to 1.1953125
- p_cols: int32 [128, 10], P('row', 'col'), may hold values from 0 to 127, as said below
- keep_cols: int32 [128, 24], P('row', 'col'), may hold values from -1 to 127, as said below
Outputs:
- purified: bfloat16 [128, 24, 128, 128], P(('row', 'layer'), 'col')
Inputs may be any that keep to these rules, and one draw needn't show every extreme that they name: `p_cols`: slot s of a block row lies in column panel s // 5, where block column k belongs to panel (k mod 16) // 8. The columns of a block row are distinct, and every block row holds its own diagonal block. `keep_cols`: slots t of a block row for panel t // 12 hold distinct block columns of that panel, followed by -1 in the unused slots; each block row uses 2 or more slots of every panel, and the first block row of every index of row uses all 12 slots of every panel.
All inputs are finite; a program needn't handle non-finite values.
Results may differ from a plain program's by a relative error of at most 0.0048.
Values may be sent and summed in bfloat16 or wider, within the bound.
A program may use at most 320 MiB of HBM per device.

v0:
```python
import jax
import jax.numpy as jnp
from jax import lax
from jax.sharding import PartitionSpec as P


def spread(value, axis, source):
    kept = jnp.where(lax.axis_index(axis) == source, value, 0).astype(value.dtype)
    return lax.psum(kept, axis)


def contract(
    left_blocks, left_cols, keep_rows, right_blocks, right_cols, layer_pos, rows_dev, sub_rows
):
    groups = left_blocks.shape[0] // sub_rows

    def one_group(pieces):
        blocks, columns, wanted = pieces
        present = columns >= 0
        safe_cols = jnp.where(present, columns, layer_pos * sub_rows)
        local_row = safe_cols // rows_dev * sub_rows + safe_cols % rows_dev - layer_pos * sub_rows
        row_cols = right_cols[local_row]
        row_blocks = right_blocks[local_row]
        matches = (row_cols[:, :, :, None] == wanted[:, None, None, :]) & present[:, :, None, None]
        selector = matches.astype(jnp.bfloat16)
        picked = jnp.einsum(
            "gast,gasyz->gatyz", selector, row_blocks, preferred_element_type=jnp.bfloat16
        )
        return jnp.einsum("gaxy,gatyz->gtxz", blocks, picked, preferred_element_type=jnp.float32)

    def regroup(values):
        return values.reshape((groups, sub_rows) + values.shape[1:])

    result = lax.map(one_group, (regroup(left_blocks), regroup(left_cols), regroup(keep_rows)))
    return result.reshape((-1,) + result.shape[2:])


def shards(p_blocks, p_cols, keep_cols):
    layer_pos = lax.axis_index("layer")
    rows_dev = p_blocks.shape[0]
    sub_rows = rows_dev // lax.axis_size("layer")
    panel_blocks, panel_cols, panel_keep = (
        spread(p_blocks, "col", layer_pos),
        spread(p_cols, "col", layer_pos),
        spread(keep_cols, "col", layer_pos),
    )
    mine_blocks = lax.dynamic_slice_in_dim(p_blocks, layer_pos * sub_rows, sub_rows, 0)
    mine_cols = lax.dynamic_slice_in_dim(p_cols, layer_pos * sub_rows, sub_rows, 0)
    right_blocks, right_cols = (
        lax.all_gather(mine_blocks, "row", axis=0, tiled=True),
        lax.all_gather(mine_cols, "row", axis=0, tiled=True),
    )
    square_part = contract(
        panel_blocks, panel_cols, keep_cols, right_blocks, right_cols, layer_pos, rows_dev, sub_rows
    )
    square_mine = lax.psum_scatter(square_part, "layer", scatter_dimension=0, tiled=True)
    square_rows = lax.all_gather(square_mine.astype(jnp.bfloat16), "layer", axis=0, tiled=True)
    square_panel = spread(square_rows, "col", layer_pos)
    cube_part = contract(
        square_panel, panel_keep, keep_cols, right_blocks, right_cols, layer_pos, rows_dev, sub_rows
    )
    cube_mine = lax.psum_scatter(cube_part, "layer", scatter_dimension=0, tiled=True)
    return (3.0 * square_mine - 2.0 * cube_mine).astype(jnp.bfloat16)


def solution(mesh):
    placed = (P("row", "col", None, None), P("row", "col"), P("row", "col"))
    return jax.shard_map(
        shards,
        mesh=mesh,
        in_specs=placed,
        out_specs=P(("row", "layer"), "col", None, None),
        check_vma=False,
    )
```

profile of v0, /device:TPU:0, one launch (start us, length us, event | category | flops | bytes accessed | tf_op | source)
XLA Modules:
  0.0 683.5 jit_solution(14193343172552070938)
XLA Ops:
  7.4 0.0 all-reduce.4.cloned.1.call-start
  7.4 3.6 broadcast_select_fusion.1
  10.9 0.0 all-reduce.4.cloned.1.call-update
  11.0 0.0 all-gather.3.cloned.1.call-start
  11.0 1.2 constant_dynamic-slice_fusion.1
  12.3 0.0 all-gather.3.cloned.1.call-update
  12.3 0.0 reduce-scatter.3.cloned.1.call-start
  12.3 0.1 constant_dynamic-slice_fusion.2
  12.4 0.1 copy.45
  12.5 0.1 reshape.264
  12.6 32.5 %all_gather.9 = s32[64,5]{1,0:T(8,128)S(1)} all-gather(s32[8,5]{1,0:T(8,128)S(1)} %copy.45), channel_id=1, replica_groups=mesh['row'=8,'col'=2,'layer'=2] {'row'}, dimensions={0}, use_global_device_ids=true | all-gather | bytes 1440 | tf_op jit(solution)/shard_map/all_gather | solution.py:51
  45.1 7.8 %all-reduce = (s32[2,8,12]{2,1,0:T(8,128)}, s32[2,8,5]{1,0,2:T(2,128)S(1)}) all-reduce(s32[2,8,12]{2,1,0:T(8,128)S(1)} %select_bitcast_fusion, s32[2,8,5]{1,0,2:T(2,128)S(1)} %reshape.264), channel_id=1, replica_groups=mesh['row'=8,'col'=2,'layer'=2] {'col'}, use_global_device_ids=true, to_apply=%region_6.7 | all-reduce | flops 272 | bytes 2176 | tf_op jit(solution)/shard_map/psum | solution.py:9
  52.9 34.9 %all-reduce.4.cloned.1.call-done = bf16[2,8,5,128,128]{4,3,2,1,0:T(8,128)(2,1)} async-done(((bf16[2,8,5,128,128]{4,3,2,1,0:T(8,128)(2,1)}), bf16[2,8,5,128,128]{4,3,2,1,0:T(8,128)(2,1)}) %all-reduce.4.cloned.1.call-update) | async-done | bytes 2621456 | tf_op jit(solution)/shard_map/psum | solution.py:9
  87.8 78.8 %all-gather.3.cloned.1.call-done = bf16[64,5,128,128]{3,2,1,0:T(8,128)(2,1)} async-done(((bf16[8,5,128,128]{3,2,1,0:T(8,128)(2,1)}), bf16[64,5,128,128]{3,2,1,0:T(8,128)(2,1)}) %all-gather.3.cloned.1.call-update) | async-done | bytes 10485776 | tf_op jit(solution)/shard_map/all_gather | solution.py:50
  166.6 6.1 broadcast.387.clone2
  172.7 100.0 %while.24 = (s32[]{:T(128)}, f32[2,8,12,128,128]{4,3,2,1,0:T(8,128)}, s32[2,8,5]{1,0,2:T(2,128)S(1)}, s32[]{:T(128)}, s32[64,5]{1,0:T(8,128)S(1)}, /*index=5*/s3...) while((s32[]{:T(128)}, ...), condition=%wide.region_3.4_spmd, body=%wide.region_2.3_spmd.sunk | while | flops 2091916032 | bytes 94383896 | solution.py:34
  172.7 0.1 copy.69
  172.8 0.1 reshape.331
  172.9 9.2 %gather_fusion = bf16[40,5,128,128]{3,2,1,0:T(8,128)(2,1)} fusion(bf16[64,5,128,128]{3,2,1,0:T(8,128)(2,1)} %get-tuple-element.405, s32[1024]{0:T(1024)S(1)} %pad_clamp_fusion.4), kind=kCustom, calls=%fused_computation.1.clone.1 | custom fusion | bytes 13107360 | tf_op jit(solution)/shard_map/while/body/eval_jaxpr/gather | solution.py:23
  182.1 0.6 gather_fusion.1
  182.7 0.1 copy.70
  182.8 14.6 %fusion.61 = bf16[8,5,12,128,128]{4,2,3,1,0:T(8,128)(2,1)} fusion(bf16[8,5,5,128,128]{4,3,2,1,0:T(8,128)(2,1)} %bitcast.100, s32[8,12]{1,0:T(8,128)S(1)} %dynamic-slice_bitcast_fusion.4, s32[8,5,5]{2,1,0:T(8,128)S(1)} %reshape.332, pred[8,5]{1,0:T(8,128)(4,1)S(1)} %compare_bitcast_fusion.4), kind=kOutput, calls=%fused_computation.6.clone.1 | convolution fusion | flops 78648000 | bytes 22283464 | tf_op jit(solution)/shard_map/while/body/eval_jaxpr/gast,gasyz->gatyz/dot_general | solution.py:26
  197.4 12.5 %fusion.62 = f32[1,8,12,128,128]{3,4,2,1,0:T(8,128)} fusion(bf16[8,5,12,128,128]{4,2,3,1,0:T(8,128)(2,1)} %fusion.61, bf16[2,8,5,128,128]{4,3,2,1,0:T(8,128)(2,1)S(1)} %copy-done.4, s32[]{:T(128)} %get-tuple-element.390), kind=kOutput, calls=%fused_computation.8.clone.1 | convolution fusion | flops 2013265920 | bytes 23330820 | tf_op jit(solution)/shard_map/while/body/eval_jaxpr/gaxy,gatyz->gtxz/dot_general | solution.py:29
  209.9 6.6 copy.71
  216.5 6.2 constant_dynamic-update-slice_fusion.4
  222.7 0.1 copy.69
  222.8 0.1 reshape.331
  222.9 9.2 %gather_fusion = bf16[40,5,128,128]{3,2,1,0:T(8,128)(2,1)} fusion(bf16[64,5,128,128]{3,2,1,0:T(8,128)(2,1)} %get-tuple-element.405, s32[1024]{0:T(1024)S(1)} %pad_clamp_fusion.4), kind=kCustom, calls=%fused_computation.1.clone.1 | custom fusion | bytes 13107360 | tf_op jit(solution)/shard_map/while/body/eval_jaxpr/gather | solution.py:23
  232.2 0.6 gather_fusion.1
  232.7 0.1 copy.70
  232.8 14.6 %fusion.61 = bf16[8,5,12,128,128]{4,2,3,1,0:T(8,128)(2,1)} fusion(bf16[8,5,5,128,128]{4,3,2,1,0:T(8,128)(2,1)} %bitcast.100, s32[8,12]{1,0:T(8,128)S(1)} %dynamic-slice_bitcast_fusion.4, s32[8,5,5]{2,1,0:T(8,128)S(1)} %reshape.332, pred[8,5]{1,0:T(8,128)(4,1)S(1)} %compare_bitcast_fusion.4), kind=kOutput, calls=%fused_computation.6.clone.1 | convolution fusion | flops 78648000 | bytes 22283464 | tf_op jit(solution)/shard_map/while/body/eval_jaxpr/gast,gasyz->gatyz/dot_general | solution.py:26
  247.4 12.5 %fusion.62 = f32[1,8,12,128,128]{3,4,2,1,0:T(8,128)} fusion(bf16[8,5,12,128,128]{4,2,3,1,0:T(8,128)(2,1)} %fusion.61, bf16[2,8,5,128,128]{4,3,2,1,0:T(8,128)(2,1)S(1)} %copy-done.4, s32[]{:T(128)} %get-tuple-element.390), kind=kOutput, calls=%fused_computation.8.clone.1 | convolution fusion | flops 2013265920 | bytes 23330820 | tf_op jit(solution)/shard_map/while/body/eval_jaxpr/gaxy,gatyz->gtxz/dot_general | solution.py:29
  260.0 6.6 copy.71
  266.5 6.2 constant_dynamic-update-slice_fusion.4
  272.7 0.0 reduce-scatter.3.cloned.1.call-update
  272.7 0.0 all-gather.5.cloned.1.call-start
  272.8 19.8 %reduce-scatter.3.cloned.1.call-done = f32[8,12,128,128]{3,2,1,0:T(8,128)} async-done(((f32[16,12,128,128]{3,2,1,0:T(8,128)}), f32[8,12,128,128]{3,2,1,0:T(8,128)}) %reduce-scatter.3.cloned.1.call-update) | async-done | bytes 6291472 | tf_op jit(solution)/shard_map/reduce_scatter | solution.py:56
  292.6 5.1 convert_element_type.12
  297.7 0.0 all-gather.5.cloned.1.call-update
  297.7 0.0 all-reduce.6.cloned.1.call-start
  297.8 18.1 %all-gather.5.cloned.1.call-done = bf16[16,12,128,128]{3,2,1,0:T(8,128)(2,1)} async-done(((bf16[8,12,128,128]{3,2,1,0:T(8,128)(2,1)}), bf16[16,12,128,128]{3,2,1,0:T(8,128)(2,1)}) %all-gather.5.cloned.1.call-update) | async-done | bytes 6291472 | tf_op jit(solution)/shard_map/all_gather | solution.py:57
  315.8 5.8 broadcast_select_fusion
  321.7 0.0 all-reduce.6.cloned.1.call-update
  321.7 0.2 reduce-scatter.5.cloned.1.call-start
  321.9 154.2 %all-reduce.6.cloned.1.call-done = bf16[2,8,12,128,128]{4,3,2,1,0:T(8,128)(2,1)} async-done(((bf16[2,8,12,128,128]{4,3,2,1,0:T(8,128)(2,1)}), bf16[2,8,12,128,128]{4,3,2,1,0:T(8,128)(2,1)}) %all-reduce.6.cloned.1.call-update) | async-done | bytes 6291472 | tf_op jit(solution)/shard_map/psum | solution.py:9
  476.2 6.2 broadcast.387.clone
  482.3 164.4 %while.25 = (s32[]{:T(128)}, f32[2,8,12,128,128]{4,3,2,1,0:T(8,128)}, s32[2,8,12]{2,1,0:T(8,128)S(1)}, s32[]{:T(128)}, s32[64,5]{1,0:T(8,128)S(1)}, /*index=5*/s...) while((s32[]{:T(128)}, ...), condition=%wide.region_8.9_spmd, body=%wide.region_7.8_spmd.sunk | while | flops 5020597248 | bytes 169888560 | solution.py:34
  482.4 0.1 reshape.337
  482.4 12.0 %gather_fusion.2 = bf16[96,5,128,128]{3,2,1,0:T(8,128)(2,1)} fusion(bf16[64,5,128,128]{3,2,1,0:T(8,128)(2,1)} %get-tuple-element.432, s32[1024]{0:T(1024)S(1)} %pad_clamp_fusion.5), kind=kCustom, calls=%fused_computation.3.clone.1 | custom fusion | bytes 31457664 | tf_op jit(solution)/shard_map/while/body/eval_jaxpr/gather | solution.py:23
  494.4 0.6 gather_fusion.3
  495.1 30.0 %fusion.67 = bf16[8,12,12,128,128]{4,2,3,1,0:T(8,128)(2,1)} fusion(bf16[8,12,5,128,128]{4,3,2,1,0:T(8,128)(2,1)} %bitcast.99, s32[8,12]{1,0:T(8,128)S(1)} %dynamic-slice_bitcast_fusion.5, s32[8,12,5]{2,1,0:T(8,128)S(1)} %reshape.338, pred[8,12]{1,0:T(8,128)(4,1)S(1)} %compare_bitcast_fusion.5), kind=kOutput, calls=%fused_computation.33.clone.2 | convolution fusion | flops 188755200 | bytes 53479776 | tf_op jit(solution)/shard_map/while/body/eval_jaxpr/gast,gasyz->gatyz/dot_general | solution.py:26
  525.0 26.8 %fusion.68 = f32[1,8,12,128,128]{3,4,2,1,0:T(8,128)} fusion(bf16[2,8,12,128,128]{4,3,2,1,0:T(8,128)(2,1)} %get-tuple-element.433, s32[]{:T(128)} %get-tuple-element.417, bf16[8,12,12,128,128]{4,2,3,1,0:T(8,128)(2,1)} %fusion.67), kind=kOutput, calls=%fused_computation.37.clone.1 | convolution fusion | flops 4831838208 | bytes 59769344 | tf_op jit(solution)/shard_map/while/body/eval_jaxpr/gaxy,gatyz->gtxz/dot_general | solution.py:29
  551.8 6.6 copy.74
  558.4 6.2 constant_dynamic-update-slice_fusion.5
  564.6 0.1 reshape.337
  564.7 11.9 %gather_fusion.2 = bf16[96,5,128,128]{3,2,1,0:T(8,128)(2,1)} fusion(bf16[64,5,128,128]{3,2,1,0:T(8,128)(2,1)} %get-tuple-element.432, s32[1024]{0:T(1024)S(1)} %pad_clamp_fusion.5), kind=kCustom, calls=%fused_computation.3.clone.1 | custom fusion | bytes 31457664 | tf_op jit(solution)/shard_map/while/body/eval_jaxpr/gather | solution.py:23
  576.6 0.6 gather_fusion.3
  577.3 30.0 %fusion.67 = bf16[8,12,12,128,128]{4,2,3,1,0:T(8,128)(2,1)} fusion(bf16[8,12,5,128,128]{4,3,2,1,0:T(8,128)(2,1)} %bitcast.99, s32[8,12]{1,0:T(8,128)S(1)} %dynamic-slice_bitcast_fusion.5, s32[8,12,5]{2,1,0:T(8,128)S(1)} %reshape.338, pred[8,12]{1,0:T(8,128)(4,1)S(1)} %compare_bitcast_fusion.5), kind=kOutput, calls=%fused_computation.33.clone.2 | convolution fusion | flops 188755200 | bytes 53479776 | tf_op jit(solution)/shard_map/while/body/eval_jaxpr/gast,gasyz->gatyz/dot_general | solution.py:26
  607.2 26.7 %fusion.68 = f32[1,8,12,128,128]{3,4,2,1,0:T(8,128)} fusion(bf16[2,8,12,128,128]{4,3,2,1,0:T(8,128)(2,1)} %get-tuple-element.433, s32[]{:T(128)} %get-tuple-element.417, bf16[8,12,12,128,128]{4,2,3,1,0:T(8,128)(2,1)} %fusion.67), kind=kOutput, calls=%fused_computation.37.clone.1 | convolution fusion | flops 4831838208 | bytes 59769344 | tf_op jit(solution)/shard_map/while/body/eval_jaxpr/gaxy,gatyz->gtxz/dot_general | solution.py:29
  634.0 6.6 copy.74
  640.5 6.2 constant_dynamic-update-slice_fusion.5
  646.7 0.0 reduce-scatter.5.cloned.1.call-update
  646.8 21.8 %reduce-scatter.5.cloned.1.call-done = f32[8,12,128,128]{3,2,1,0:T(8,128)} async-done(((f32[16,12,128,128]{3,2,1,0:T(8,128)}), f32[8,12,128,128]{3,2,1,0:T(8,128)}) %reduce-scatter.5.cloned.1.call-update) | async-done | bytes 6291472 | tf_op jit(solution)/shard_map/reduce_scatter | solution.py:62
  668.6 7.8 %subtract_convert_fusion = bf16[8,12,128,128]{3,2,1,0:T(8,128)(2,1)} fusion(f32[8,12,128,128]{3,2,1,0:T(8,128)} %reduce-scatter.5.cloned.1.call-done, f32[8,12,128,128]{3,2,1,0:T(8,128)} %reduce-scatter.3.cloned.1.call-done), kind=kLoop, calls=%fused_computation.64 | loop fusion | flops 6291456 | bytes 15728640 | tf_op jit(solution)/shard_map/convert_element_type | solution.py:63
  (34 shorter events, 0.3 us)
Async XLA Ops:
  7.4 3.6 copy-start
  7.4 5.0 copy-start.3
  7.4 37.7 %copy-start.1 = (s32[16,12]{1,0:T(8,128)S(1)}, s32[16,12]{1,0:T(8,128)}, u32[]{:S(2)}) copy-start(s32[16,12]{1,0:T(8,128)} %param.9) | copy-start | bytes 2308
  7.4 80.5 %all-reduce.4.cloned.1.call-start = ((), (), s32[]{:S(2)}) async-start(), calls=%async_computation.3 | async-start | bytes 5242880 | tf_op jit(solution)/shard_map/psum | solution.py:9
  11.0 155.6 %all-gather.3.cloned.1.call-start = ((), (), s32[]{:S(2)}) async-start(), calls=%async_computation.2 | async-start | bytes 11796480 | tf_op jit(solution)/shard_map/all_gather | solution.py:50
  12.3 280.3 %reduce-scatter.3.cloned.1.call-start = ((), (), s32[]{:S(2)}) async-start(), calls=%async_computation.4 | async-start | bytes 18874368 | tf_op jit(solution)/shard_map/reduce_scatter | solution.py:56
  182.8 14.6 %copy-start.4 = (bf16[2,8,5,128,128]{4,3,2,1,0:T(8,128)(2,1)S(1)}, bf16[2,8,5,128,128]{4,3,2,1,0:T(8,128)(2,1)}, u32[]{:S(2)}) copy-start(bf16[2,8,5,128,128]{4,3,2,1,0:T(8,128)(2,1)} %get-tuple-element.406) | copy-start | bytes 7864324 | tf_op jit(solution)/shard_map/while
  232.8 14.6 %copy-start.4 = (bf16[2,8,5,128,128]{4,3,2,1,0:T(8,128)(2,1)S(1)}, bf16[2,8,5,128,128]{4,3,2,1,0:T(8,128)(2,1)}, u32[]{:S(2)}) copy-start(bf16[2,8,5,128,128]{4,3,2,1,0:T(8,128)(2,1)} %get-tuple-element.406) | copy-start | bytes 7864324 | tf_op jit(solution)/shard_map/while
  272.7 43.1 %all-gather.5.cloned.1.call-start = ((), (), s32[]{:S(2)}) async-start(), calls=%async_computation.5 | async-start | bytes 9437184 | tf_op jit(solution)/shard_map/all_gather | solution.py:57
  297.7 178.4 %all-reduce.6.cloned.1.call-start = ((), (), s32[]{:S(2)}) async-start(), calls=%async_computation.6 | async-start | bytes 12582912 | tf_op jit(solution)/shard_map/psum | solution.py:9
  321.7 160.6 %copy-start.2 = (s32[2,8,12]{2,1,0:T(8,128)S(1)}, s32[2,8,12]{2,1,0:T(8,128)}, u32[]{:S(2)}) copy-start(s32[2,8,12]{2,1,0:T(8,128)} %get-tuple-element.410) | copy-start | bytes 2308
  321.7 346.8 %reduce-scatter.5.cloned.1.call-start = ((), (), s32[]{:S(2)}) async-start(), calls=%async_computation.7 | async-start | bytes 18874368 | tf_op jit(solution)/shard_map/reduce_scatter | solution.py:62
Sparse Core Ops, SparseCore 0:
  11.1 76.7 all-reduce.3
  272.8 19.6 reduce-scatter.2
  297.9 17.9 all-gather.4
  321.8 154.3 all-reduce.5
  646.9 21.6 reduce-scatter.4
Sparse Core Ops, SparseCore 1:
  13.9 152.7 all-gather.2
where the time goes:
time: 684 us; the launch traced here: 683 us
  waiting for transfers between devices  328 us (48%)
  matrix products  168 us (25%)
  local copies, waits for them, and re-layouts  110 us (16%)
  blocking collectives  40.4 us (6%)
  other arithmetic  22.5 us (3%)
  between operations  14.6 us (2%)
    psum x2, waiting for transfers between devices, spread(): return lax.psum(kept, axis)  189 us
    dot_general x4, matrix products, one_group(): jnp.einsum('gast,gasyz->gatyz', selector, row_blocks, preferred_element_t...  89.1 us
    all_gather x1, waiting for transfers between devices, shards(): lax.all_gather(mine_blocks, 'row', axis=0, tiled=True)  78.8 us
    dot_general x4, matrix products, one_group(): jnp.einsum('gaxy,gatyz->gtxz', blocks, picked, preferred_element_type=jnp...  78.6 us
    dynamic_update_slice x8, local copies, waits for them, and re-layouts, contract(): lax.map(one_group, (regroup(left_blocks), regroup(left_cols), regroup(kee...  51.1 us
    gather x4, local copies, waits for them, and re-layouts, one_group(): row_blocks = right_blocks[local_row]  42.3 us
    all_gather x1, blocking collectives, shards(): lax.all_gather(mine_cols, 'row', axis=0, tiled=True)  32.5 us
    reduce_scatter x1, waiting for transfers between devices, shards(): lax.psum_scatter(cube_part, 'layer', scatter_dimension=0, tiled=True)  21.8 us
  transfers between devices with their start and end apart: 6, of which 6 were waited for; matrix products, arithmetic and copies ran while one was open for 0% of the time, Pallas kernels for 0%

commit v1 on v0

v1 whole, which is shorter than its diff:
```python
import functools

import jax
import jax.numpy as jnp
from jax import lax
from jax.experimental import pallas as pl
from jax.experimental.pallas import tpu as pltpu
from jax.sharding import PartitionSpec as P

MESH = pl.DeviceIdType.MESH
LANES = 128
DEPTH = 16
GROUP = 4


def gather_kernel(
    n_row,
    lines,
    blocks_ref,
    meta_ref,
    full_ref,
    table_ref,
    other_ref,
    other_meta_ref,
    z_send,
    z_recv,
    y_send,
    y_recv,
    c_send,
    c_recv,
    m_send,
    m_recv,
    x_send,
    x_recv,
    local,
):
    row, col, layer = lax.axis_index("row"), lax.axis_index("col"), lax.axis_index("layer")
    length = n_row // 2
    z, y = row // 2, row % 2
    half = blocks_ref.shape[0] // 2
    mine = pl.ds(pl.multiple_of(layer * half, half), half)
    theirs = pl.ds(pl.multiple_of((1 - layer) * half, half), half)
    parts = len(lines)

    barrier = pltpu.get_barrier_semaphore()
    for step in range(1, n_row):
        pl.semaphore_signal(
            barrier, inc=1, device_id=(lax.rem(row + step, n_row), col, layer), device_id_type=MESH
        )
    pl.semaphore_signal(barrier, inc=1, device_id=(row, 1 - col, layer), device_id_type=MESH)
    pl.semaphore_signal(barrier, inc=1, device_id=(row, col, 1 - layer), device_id_type=MESH)
    pl.semaphore_wait(barrier, n_row + 1)

    def source(part, chunk):
        lo, hi = lines[part]
        if chunk is None:
            return blocks_ref.at[mine, pl.ds(lo, hi - lo)]
        return full_ref.at[chunk, mine, pl.ds(lo, hi - lo)]

    def target(part, chunk, rows):
        lo, hi = lines[part]
        return full_ref.at[chunk, rows, pl.ds(lo, hi - lo)]

    def z_copy(part, pos, way, own):
        chunk = pos * 2 + y
        return pltpu.make_async_remote_copy(
            src_ref=source(part, None if own else chunk),
            dst_ref=target(part, chunk, mine),
            send_sem=z_send.at[part, way, pos],
            recv_sem=z_recv.at[part, pos],
            device_id=(row + (2 if way else -2), col, layer),
            device_id_type=MESH,
        )

    def y_copy(part, pos, own, arriving=False):
        chunk = pos * 2 + (1 - y if arriving else y)
        return pltpu.make_async_remote_copy(
            src_ref=source(part, None if own else chunk),
            dst_ref=target(part, chunk, mine),
            send_sem=y_send.at[part, pos],
            recv_sem=y_recv.at[part, pos],
            device_id=(z * 2 + 1 - y, col, layer),
            device_id_type=MESH,
        )

    def c_copy(part, chunk, arriving=False):
        return pltpu.make_async_remote_copy(
            src_ref=source(part, chunk),
            dst_ref=target(part, chunk, theirs if arriving else mine),
            send_sem=c_send.at[part, chunk],
            recv_sem=c_recv.at[part, chunk],
            device_id=(row, col, 1 - layer),
            device_id_type=MESH,
        )

    def m_copy(step, arriving=False):
        return pltpu.make_async_remote_copy(
            src_ref=meta_ref,
            dst_ref=table_ref.at[lax.rem(row - step + n_row, n_row) if arriving else row],
            send_sem=m_send.at[step],
            recv_sem=m_recv.at[step],
            device_id=(lax.rem(row + step, n_row), col, layer),
            device_id_type=MESH,
        )

    x_block = pltpu.make_async_remote_copy(
        src_ref=blocks_ref.at[mine],
        dst_ref=other_ref,
        send_sem=x_send.at[0],
        recv_sem=x_recv.at[0],
        device_id=(row, 1 - col, layer),
        device_id_type=MESH,
    )
    x_meta = pltpu.make_async_remote_copy(
        src_ref=meta_ref,
        dst_ref=other_meta_ref,
        send_sem=x_send.at[1],
        recv_sem=x_recv.at[1],
        device_id=(row, 1 - col, layer),
        device_id_type=MESH,
    )

    def go_right(pos):
        return pl.when(z < length - 1)

    for part in range(parts):
        y_copy(part, z, True).start()

        @pl.when(z < length - 1)
        def _():
            z_copy(part, z, 1, True).start()

        @pl.when(z > 0)
        def _():
            z_copy(part, z, 0, True).start()

    x_block.start()
    x_meta.start()
    for step in range(1, n_row):
        m_copy(step).start()
    own_blocks = pltpu.make_async_copy(blocks_ref, full_ref.at[row], local.at[0])
    own_meta = pltpu.make_async_copy(meta_ref, table_ref.at[row], local.at[1])
    own_blocks.start()
    own_meta.start()

    def from_side(part, pos, way):
        z_copy(part, pos, way, False).wait_recv()
        y_copy(part, pos, False).start()

        @pl.when((z < length - 1) if way else (z > 0))
        def _():
            z_copy(part, pos, way, False).start()

        c_copy(part, pos * 2 + y).start()

    def from_y(part, pos):
        y_copy(part, pos, False, True).wait_recv()
        c_copy(part, pos * 2 + 1 - y).start()

    for step in range(1, length + 1):
        for part in range(parts):
            if step < length:

                @pl.when(z - step >= 0)
                def _():
                    from_side(part, z - step, 1)

                @pl.when(z + step < length)
                def _():
                    from_side(part, z + step, 0)

        for part in range(parts):
            if step == 1:
                from_y(part, z)
            else:

                @pl.when(z - step + 1 >= 0)
                def _():
                    from_y(part, z - step + 1)

                @pl.when(z + step - 1 < length)
                def _():
                    from_y(part, z + step - 1)

    for step in range(1, n_row):
        m_copy(step, True).wait_recv()
        m_copy(step).wait_send()
    x_block.wait()
    x_meta.wait()
    own_blocks.wait()
    own_meta.wait()

    for part in range(parts):
        for pos in range(length):
            y_copy(part, pos, False).wait_send()

            @pl.when((pos <= z) & (z < length - 1))
            def _():
                z_copy(part, pos, 1, False).wait_send()

            @pl.when((pos >= z) & (z > 0))
            def _():
                z_copy(part, pos, 0, False).wait_send()

        for chunk in range(n_row):

            @pl.when(chunk != row)
            def _():
                c_copy(part, chunk).wait_send()
                c_copy(part, chunk, True).wait_recv()


def gather(blocks, meta, n_row):
    rows, slots = blocks.shape[:2]
    middle = slots // 2
    lines = ((0, middle), (middle, slots))
    parts = len(lines)
    length = n_row // 2
    anywhere = pl.BlockSpec(memory_space=pl.ANY)
    dma = pltpu.SemaphoreType.DMA
    return pl.pallas_call(
        functools.partial(gather_kernel, n_row, lines),
        out_shape=(
            jax.ShapeDtypeStruct((n_row,) + blocks.shape, blocks.dtype),
            jax.ShapeDtypeStruct((n_row,) + meta.shape, meta.dtype),
            jax.ShapeDtypeStruct((rows // 2,) + blocks.shape[1:], blocks.dtype),
            jax.ShapeDtypeStruct(meta.shape, meta.dtype),
        ),
        in_specs=[anywhere] * 2,
        out_specs=[anywhere] * 4,
        scratch_shapes=[
            dma((parts, 2, length)),
            dma((parts, length)),
            dma((parts, length)),
            dma((parts, length)),
            dma((parts, n_row)),
            dma((parts, n_row)),
            dma((n_row,)),
            dma((n_row,)),
            dma((2,)),
            dma((2,)),
            dma((2,)),
        ],
        compiler_params=pltpu.CompilerParams(collective_id=0, has_side_effects=True),
        name="gather",
    )(blocks, meta)


def list_products(left_cols, count, per_row, cols, slots, keep, keeps, inverse, sub_rows, found):
    width = inverse.shape[0] // sub_rows

    def clear(at, carry):
        for k in range(8):
            inverse[at * 8 + k] = -1
        return carry

    def mark(at, carry):
        column = keep[at]

        @pl.when(column >= 0)
        def _():
            inverse[at // keeps * width + jnp.maximum(column, 0)] = at

        return carry

    lax.fori_loop(0, inverse.shape[0] // 8, clear, 0)
    lax.fori_loop(0, sub_rows * keeps, mark, 0)
    lefts, rights, results = found

    def one(at, total):
        column = left_cols[at]
        present = column >= 0
        base = jnp.maximum(column, 0) * slots
        line = at // per_row * width
        for a in range(slots):
            result = inverse[line + cols[base + a]]
            lefts[total] = at
            rights[total] = base + a
            results[total] = result
            total = total + jnp.where(present & (result >= 0), 1, 0)
        return total

    return lax.fori_loop(0, count, one, 0)


def multiply(total, load_left, right_hbm, acc, spare, found, buffers, sems):
    lefts, rights, results = found
    for k in range(GROUP):
        lefts[total + k] = 0
        rights[total + k] = 0
        results[total + k] = spare
    groups = (total + GROUP - 1) // GROUP
    ahead = DEPTH // GROUP

    def copies(group, go):
        slot = lax.rem(group, ahead) * GROUP
        for k in range(GROUP):
            copy = pltpu.make_async_copy(
                right_hbm.at[rights[group * GROUP + k]], buffers.at[slot + k], sems.at[slot + k]
            )
            if go:
                copy.start()
            else:
                copy.wait()
        return slot

    def prime(group, carry):
        copies(group, True)
        return carry

    lax.fori_loop(0, jnp.minimum(groups, ahead), prime, 0)

    def step(group, carry):
        slot = copies(group, False)
        products = [
            jnp.dot(
                load_left(lefts[group * GROUP + k]),
                buffers[slot + k],
                preferred_element_type=jnp.float32,
            )
            for k in range(GROUP)
        ]
        for k in range(GROUP):
            acc[results[group * GROUP + k]] += products[k]

        @pl.when(group + ahead < groups)
        def _():
            copies(group + ahead, True)

        return carry

    lax.fori_loop(0, groups, step, 0)


def square_kernel(
    dims, left_cols, cols, keep, left, right, out, half, acc, buffers, l1, l2, l3, inverse, sems
):
    sub_rows, slots, keeps = dims
    count = sub_rows * keeps
    acc[...] = jnp.zeros_like(acc)
    found = (l1, l2, l3)
    total = list_products(
        left_cols, left.shape[0], left.shape[0] // sub_rows, cols, slots, keep, keeps, inverse, sub_rows, found
    )
    multiply(total, lambda at: left[at], right, acc, count, found, buffers, sems)

    def finish(at, carry):
        value = acc[at]
        out[at] = value
        half[at] = value.astype(half.dtype)
        return carry

    lax.fori_loop(0, count, finish, 0)


def cube_kernel(
    dims, left_cols, cols, keep, left, right, base, out, acc, buffers, l1, l2, l3, inverse, sems, *, scale
):
    sub_rows, slots, keeps = dims
    count = sub_rows * keeps
    acc[...] = jnp.zeros_like(acc)
    found = (l1, l2, l3)
    total = list_products(
        left_cols, left.shape[0], left.shape[0] // sub_rows, cols, slots, keep, keeps, inverse, sub_rows, found
    )
    multiply(total, lambda at: left[at], right, acc, count, found, buffers, sems)

    def finish(at, carry):
        out[at] = (scale * base[at] - 2.0 * acc[at]).astype(out.dtype)
        return carry

    lax.fori_loop(0, count, finish, 0)


def products(kernel, outs, dims, left_cols, cols, keep, left, right, extra, width, name):
    sub_rows, slots, keeps = dims
    block = left.shape[1:]
    count = sub_rows * keeps
    entries = left.shape[0] * slots + GROUP
    smem = pl.BlockSpec(memory_space=pltpu.SMEM)
    vmem = pl.BlockSpec(memory_space=pltpu.VMEM)
    hbm = pl.BlockSpec(memory_space=pltpu.HBM)
    scalars = pltpu.SMEM((entries,), jnp.int32)
    return pl.pallas_call(
        functools.partial(kernel, dims),
        out_shape=tuple(jax.ShapeDtypeStruct((count,) + block, t) for t in outs),
        in_specs=[smem] * 3 + [vmem, hbm] + [vmem] * len(extra),
        out_specs=tuple(vmem for _ in outs),
        scratch_shapes=[
            pltpu.VMEM((count + 1,) + block, jnp.float32),
            pltpu.VMEM((DEPTH,) + block, right.dtype),
            scalars,
            scalars,
            scalars,
            pltpu.SMEM((sub_rows * width,), jnp.int32),
            pltpu.SemaphoreType.DMA((DEPTH,)),
        ],
        compiler_params=pltpu.CompilerParams(vmem_limit_bytes=48 * 1024 * 1024),
        cost_estimate=pl.CostEstimate(
            flops=2 * 2 * count * 128**3, bytes_accessed=30_000_000, transcendentals=0
        ),
        name=name,
    )(left_cols, cols, keep, left, right, *extra)


def shards(p_blocks, p_cols, keep_cols):
    n_row = lax.axis_size("row")
    layer = lax.axis_index("layer")
    rows, slots = p_blocks.shape[:2]
    block = p_blocks.shape[2:]
    keeps = keep_cols.shape[1]
    sub_rows = rows // lax.axis_size("layer")
    width = n_row * rows
    dims = (sub_rows, slots, keeps)

    unused = jnp.zeros((rows, LANES - slots - keeps), jnp.int32)
    meta = jnp.concatenate([p_cols, keep_cols, unused], axis=1)
    full, table, other_blocks, other_meta = gather(p_blocks, meta, n_row)

    def own(values):
        return lax.dynamic_slice_in_dim(values, layer * sub_rows, sub_rows, 0)

    right = full.reshape((width * slots,) + block)
    cols = table[:, :, :slots].reshape(-1)
    meta_here, meta_there = own(meta), own(other_meta)
    keep_here = meta_here[:, slots : slots + keeps].reshape(-1)
    keep_there = meta_there[:, slots : slots + keeps].reshape(-1)
    left = jnp.concatenate([own(p_blocks), other_blocks], axis=1).reshape((-1,) + block)
    left_cols = jnp.concatenate([meta_here[:, :slots], meta_there[:, :slots]], axis=1).reshape(-1)

    square, half = products(
        square_kernel,
        (jnp.float32, jnp.bfloat16),
        dims,
        left_cols,
        cols,
        keep_here,
        left,
        right,
        (),
        width,
        "square",
    )
    half_there = lax.ppermute(half, "col", [(0, 1), (1, 0)])
    (partial,) = products(
        functools.partial(cube_kernel, scale=3.0),
        (jnp.float32,),
        dims,
        keep_here,
        cols,
        keep_here,
        half,
        right,
        (square,),
        width,
        "cube_here",
    )
    (result,) = products(
        functools.partial(cube_kernel, scale=1.0),
        (jnp.bfloat16,),
        dims,
        keep_there,
        cols,
        keep_here,
        half_there,
        right,
        (partial,),
        width,
        "cube_there",
    )
    return result.reshape((sub_rows, keeps) + block)


def solution(mesh):
    placed = (P("row", "col", None, None), P("row", "col"), P("row", "col"))
    return jax.shard_map(
        shards,
        mesh=mesh,
        in_specs=placed,
        out_specs=P(("row", "layer"), "col", None, None),
        check_vma=False,
    )
```

time: 684 us -> 237 us (0.35)
  waiting for transfers between devices: 328 us -> 48.8 us
  Pallas kernels: 0 us -> 178 us
  matrix products: 168 us -> 0 us
  local copies, waits for them, and re-layouts: 110 us -> 4.35 us
  blocking collectives: 40.4 us -> 0 us
  other arithmetic: 22.5 us -> 2.3 us
  between operations: 14.6 us -> 0.06 us
    psum x2 -> x0, waiting for transfers between devices: 189 us -> none  [spread(): return lax.psum(kept, axis)]
    pallas_call x0 -> x4, Pallas kernels: none -> 178 us  [the longest x1 123 us: gather(): pl.pallas_call(functools.partial(gather_kernel, n_row, lines), out_shape=...]
    dot_general x8 -> x0, matrix products: 168 us -> none  [the longest x4 89.1 us: one_group(): jnp.einsum('gast,gasyz->gatyz', selector, row_blocks, preferred_element_t...]
    all_gather x2 -> x0, waiting for transfers between devices: 96.8 us -> none  [the longest x1 78.8 us: shards(): lax.all_gather(mine_blocks, 'row', axis=0, tiled=True)]
    dynamic_update_slice x8 -> x0, local copies, waits for them, and re-layouts: 51.1 us -> none  [contract(): lax.map(one_group, (regroup(left_blocks), regroup(left_cols), regroup(kee...]
    ppermute x0 -> x1, waiting for transfers between devices: none -> 48.8 us  [shards(): half_there = lax.ppermute(half, 'col', [(0, 1), (1, 0)])]
    gather x12 -> x0, local copies, waits for them, and re-layouts: 44.7 us -> none  [the longest x4 42.3 us: one_group(): row_blocks = right_blocks[local_row]]
    reduce_scatter x2 -> x0, waiting for transfers between devices: 41.6 us -> none  [the longest x1 21.8 us: shards(): lax.psum_scatter(cube_part, 'layer', scatter_dimension=0, tiled=True)]
  transfers between devices with their start and end apart: 6 -> 1, of which waited for: 6 -> 1; matrix products, arithmetic and copies ran while one was open for 0% -> 0% of each run, Pallas kernels for 0% -> 9%
where the time goes in v1:
time: 237 us; the launch traced here: 234 us
  Pallas kernels  178 us (75%)
  waiting for transfers between devices  48.8 us (21%)
  local copies, waits for them, and re-layouts  4.35 us (2%)
    pallas_call x1, Pallas kernels, gather(): pl.pallas_call(functools.partial(gather_kernel, n_row, lines), out_shape=...  123 us
    pallas_call x3, Pallas kernels, products(): pl.pallas_call(functools.partial(kernel, dims), out_shape=tuple((jax.Shap...  54.2 us
    ppermute x1, waiting for transfers between devices, shards(): half_there = lax.ppermute(half, 'col', [(0, 1), (1, 0)])  48.8 us
  transfers between devices with their start and end apart: 1, of which 1 were waited for; matrix products, arithmetic and copies ran while one was open for 0% of the time, Pallas kernels for 9%

profile of v1, /device:TPU:0, one launch (start us, length us, event | category | flops | bytes accessed | tf_op | source)
XLA Modules:
  0.0 234.1 jit_solution(7189043081757193659)
XLA Ops:
  0.0 0.0 copy-start.1
  0.0 0.1 pad.6.clone
  0.1 0.8 copy.5
  0.8 1.4 constant_dynamic-slice_fusion
  2.3 0.0 copy-done.1
  2.3 0.7 add_add_fusion.meta_ref
  2.9 0.0 copy-start
  2.9 123.4 %gather.1 = (bf16[8,16,5,128,128]{4,3,2,1,0:T(8,128)(2,1)}, s32[8,16,128]{2,1,0:T(8,128)}, bf16[8,5,128,128]{3,2,1,0:T(8,128)(2,1)}, s32[16,128]{1,0:T(8,128)}) custom-call(bf16[16,5,128,128]{3,2,1,0:T(8,128)(2,1)} %blocks_ref.1, s32[16,128]{1,0:T(8,128)} %add_add_fusion.meta_ref), custom_call_target="tpu_custom_call" | custom-call | tf_op jit(solution)/shard_map/gather/pallas_call | solution.py:221
  126.4 0.0 copy-done
  126.4 0.7 constant_dynamic-slice_fusion.1
  127.1 1.0 reshape.22.cols
  128.1 0.1 slice.17
  128.2 0.1 pad_add_fusion
  128.3 0.1 reshape.24.left_cols
  128.4 0.1 reshape.23.keep.left_cols
  128.4 1.5 pad_maximum_fusion
  130.0 17.0 %square.1 = (f32[96,128,128]{2,1,0:T(8,128)}, bf16[96,128,128]{2,1,0:T(8,128)(2,1)S(1)}) custom-call(s32[80]{0:T(128)S(1)} %reshape.24.left_cols, s32[640]{0:T(1024)S(1)} %reshape.22.cols, s32[96]{0:T(128)S(1)} %reshape.23.keep.left_cols, bf16[80,128,128]{2,1,0:T(8,128)(2,1)S(1)} %bitcast.6, bf16[640,128,128]{2,1,0:T(8,128)(2,1)} %bitcast.7), custom_call_target="tpu_custom_call" | custom-call | flops 805306368 | bytes 30000000 | tf_op jit(solution)/shard_map/square/pallas_call | solution.py:384
  146.9 0.9 collective-permute-start
  147.9 0.1 slice.15
  148.0 0.1 reshape.21.left_cols
  148.0 20.7 %cube_here.1.base = f32[96,128,128]{2,1,0:T(8,128)} custom-call(s32[96]{0:T(128)S(1)} %reshape.23.keep.left_cols, s32[640]{0:T(1024)S(1)} %reshape.22.cols, s32[96]{0:T(128)S(1)} %reshape.23.keep.left_cols, bf16[96,128,128]{2,1,0:T(8,128)(2,1)S(1)} %get-tuple-element.15.left, bf16[640,128,128]{2,1,0:T(8,128)(2,1)} %bitcast.8, ...), custom_call_target="tpu_custom_call" | custom-call | flops 805306368 | bytes 30000000 | tf_op jit(solution)/shard_map/cube_here/pallas_call | solution.py:384
  168.7 48.8 %collective-permute-done.left = bf16[96,128,128]{2,1,0:T(8,128)(2,1)} collective-permute-done((bf16[96,128,128]{2,1,0:T(8,128)(2,1)S(1)}, bf16[96,128,128]{2,1,0:T(8,128)(2,1)}, u32[]{:S(2)}, u32[]{:S(2)}) %collective-permute-start) | collective-permute-done | bytes 3145760 | tf_op jit(solution)/shard_map/ppermute | solution.py:444
  217.5 16.6 %cube_there.1 = bf16[96,128,128]{2,1,0:T(8,128)(2,1)} custom-call(s32[96]{0:T(128)S(1)} %reshape.21.left_cols, s32[640]{0:T(1024)S(1)} %reshape.22.cols, s32[96]{0:T(128)S(1)} %reshape.23.keep.left_cols, bf16[96,128,128]{2,1,0:T(8,128)(2,1)} %collective-permute-done.left, bf16[640,128,128]{2,1,0:T(8,128)(2,1)} %bitcast.9, f32[96,128,128]{2,1,0:T(8,128)} %cube_here.1.base), custom_call_target="tpu_custom_call" | custom-call | flops 805306368 | bytes 30000000 | tf_op jit(solution)/shard_map/cube_there/pallas_call | solution.py:384
  (1 shorter events, 0.0 us)
Async XLA Ops:
  0.0 2.3 copy-start.1
  2.9 123.5 %copy-start = (s32[16,128]{1,0:T(8,128)S(1)}, s32[16,128]{1,0:T(8,128)}, u32[]{:S(2)}) copy-start(s32[16,128]{1,0:T(8,128)} %add_add_fusion.meta_ref) | copy-start | bytes 24580
  146.9 70.5 %collective-permute-start = (bf16[96,128,128]{2,1,0:T(8,128)(2,1)S(1)}, bf16[96,128,128]{2,1,0:T(8,128)(2,1)}, u32[]{:S(2)}, u32[]{:S(2)}) collective-permute-start(bf16[96,128,128]{2,1,0:T(8,128)(2,1)S(1)} %get-tuple-element.15.left), channel_id=1, source_target_pairs={{0,2},{2,0},{1,3},{3,1},{4,6},{6,4},{5,7},{7,5},{8,10},{10,8},{9,1... | collective-permute-start | bytes 9437192 | tf_op jit(solution)/shard_map/ppermute | solution.py:444

commit v2 on v1

--- a/solution.py
+++ b/solution.py
@@ -61,13 +61,12 @@
         lo, hi = lines[part]
         return full_ref.at[chunk, rows, pl.ds(lo, hi - lo)]
 
-    def z_copy(part, pos, way, own):
-        chunk = pos * 2 + y
+    def z_copy(part, chunk, way, own):
         return pltpu.make_async_remote_copy(
             src_ref=source(part, None if own else chunk),
             dst_ref=target(part, chunk, mine),
-            send_sem=z_send.at[part, way, pos],
-            recv_sem=z_recv.at[part, pos],
+            send_sem=z_send.at[part, way, chunk],
+            recv_sem=z_recv.at[part, chunk],
             device_id=(row + (2 if way else -2), col, layer),
             device_id_type=MESH,
         )
@@ -120,20 +119,23 @@
         device_id_type=MESH,
     )
 
-    def go_right(pos):
-        return pl.when(z < length - 1)
-
-    for part in range(parts):
+    straight = range(parts - 1)
+    turned = parts - 1
+
+    def to_sides(part, chunk, own):
+        @pl.when(z < length - 1)
+        def _():
+            z_copy(part, chunk, 1, own).start()
+
+        @pl.when(z > 0)
+        def _():
+            z_copy(part, chunk, 0, own).start()
+
+    y_copy(turned, z, True).start()
+    for part in straight:
         y_copy(part, z, True).start()
-
-        @pl.when(z < length - 1)
-        def _():
-            z_copy(part, z, 1, True).start()
-
-        @pl.when(z > 0)
-        def _():
-            z_copy(part, z, 0, True).start()
-
+        to_sides(part, row, True)
+    to_sides(turned, row, True)
     x_block.start()
     x_meta.start()
     for step in range(1, n_row):
@@ -143,44 +145,45 @@
     own_blocks.start()
     own_meta.start()
 
-    def from_side(part, pos, way):
-        z_copy(part, pos, way, False).wait_recv()
-        y_copy(part, pos, False).start()
+    def from_side(part, pos, way, side, on_to_y):
+        chunk = pos * 2 + side
+        z_copy(part, chunk, way, False).wait_recv()
 
         @pl.when((z < length - 1) if way else (z > 0))
         def _():
-            z_copy(part, pos, way, False).start()
-
-        c_copy(part, pos * 2 + y).start()
+            z_copy(part, chunk, way, False).start()
+
+        if on_to_y:
+            y_copy(part, pos, False).start()
+        c_copy(part, chunk).start()
 
     def from_y(part, pos):
         y_copy(part, pos, False, True).wait_recv()
         c_copy(part, pos * 2 + 1 - y).start()
 
+    def both_sides(step, act):
+        @pl.when(z - step >= 0)
+        def _():
+            act(z - step, 1)
+
+        @pl.when(z + step < length)
+        def _():
+            act(z + step, 0)
+
+    from_y(turned, z)
+    to_sides(turned, z * 2 + 1 - y, False)
     for step in range(1, length + 1):
-        for part in range(parts):
-            if step < length:
-
-                @pl.when(z - step >= 0)
-                def _():
-                    from_side(part, z - step, 1)
-
-                @pl.when(z + step < length)
-                def _():
-                    from_side(part, z + step, 0)
-
-        for part in range(parts):
+        if step < length:
+            for part in straight:
+                both_sides(step, lambda pos, way: from_side(part, pos, way, y, True))
+        if step > 1:
+            both_sides(step - 1, lambda pos, way: from_side(turned, pos, way, y, False))
+            both_sides(step - 1, lambda pos, way: from_side(turned, pos, way, 1 - y, False))
+        for part in straight:
             if step == 1:
                 from_y(part, z)
             else:
-
-                @pl.when(z - step + 1 >= 0)
-                def _():
-                    from_y(part, z - step + 1)
-
-                @pl.when(z + step - 1 < length)
-                def _():
-                    from_y(part, z + step - 1)
+                both_sides(step - 1, lambda pos, way: from_y(part, pos))
 
     for step in range(1, n_row):
         m_copy(step, True).wait_recv()
@@ -192,16 +195,20 @@
 
     for part in range(parts):
         for pos in range(length):
-            y_copy(part, pos, False).wait_send()
-
-            @pl.when((pos <= z) & (z < length - 1))
-            def _():
-                z_copy(part, pos, 1, False).wait_send()
-
-            @pl.when((pos >= z) & (z > 0))
-            def _():
-                z_copy(part, pos, 0, False).wait_send()
-
+            if part != turned:
+                y_copy(part, pos, False).wait_send()
+            for side in range(2):
+
+                @pl.when((pos <= z) & (z < length - 1) & ((part == turned) | (y == side)))
+                def _():
+                    z_copy(part, pos * 2 + side, 1, False).wait_send()
+
+                @pl.when((pos >= z) & (z > 0) & ((part == turned) | (y == side)))
+                def _():
+                    z_copy(part, pos * 2 + side, 0, False).wait_send()
+
+        if part == turned:
+            y_copy(part, z, False).wait_send()
         for chunk in range(n_row):
 
             @pl.when(chunk != row)
@@ -212,8 +219,9 @@
 
 def gather(blocks, meta, n_row):
     rows, slots = blocks.shape[:2]
-    middle = slots // 2
-    lines = ((0, middle), (middle, slots))
+    turn = slots - max(slots // 5, 1)
+    middle = turn // 2
+    lines = ((0, middle), (middle, turn), (turn, slots))
     parts = len(lines)
     length = n_row // 2
     anywhere = pl.BlockSpec(memory_space=pl.ANY)
@@ -229,8 +237,8 @@
         in_specs=[anywhere] * 2,
         out_specs=[anywhere] * 4,
         scratch_shapes=[
-            dma((parts, 2, length)),
-            dma((parts, length)),
+            dma((parts, 2, n_row)),
+            dma((parts, n_row)),
             dma((parts, length)),
             dma((parts, length)),
             dma((parts, n_row)),
@@ -332,47 +340,81 @@
     lax.fori_loop(0, groups, step, 0)
 
 
+def each_block(count, act):
+    def step(at, carry):
+        act(at)
+        return carry
+
+    lax.fori_loop(0, count, step, 0)
+
+
+def listed(dims, left_cols, cols, keep, left, found, inverse):
+    sub_rows, slots, keeps = dims
+    return list_products(
+        left_cols, left.shape[0], left.shape[0] // sub_rows, cols, slots, keep, keeps, inverse, sub_rows, found
+    )
+
+
 def square_kernel(
-    dims, left_cols, cols, keep, left, right, out, half, acc, buffers, l1, l2, l3, inverse, sems
+    dims, left_cols, cols, keep, left, right, out, half, acc, buffers, l1, l2, l3, inverse, sems, own_sem
 ):
-    sub_rows, slots, keeps = dims
-    count = sub_rows * keeps
+    count = dims[0] * dims[2]
     acc[...] = jnp.zeros_like(acc)
     found = (l1, l2, l3)
-    total = list_products(
-        left_cols, left.shape[0], left.shape[0] // sub_rows, cols, slots, keep, keeps, inverse, sub_rows, found
-    )
+    total = listed(dims, left_cols, cols, keep, left, found, inverse)
     multiply(total, lambda at: left[at], right, acc, count, found, buffers, sems)
-
-    def finish(at, carry):
-        value = acc[at]
-        out[at] = value
-        half[at] = value.astype(half.dtype)
-        return carry
-
-    lax.fori_loop(0, count, finish, 0)
-
-
-def cube_kernel(
-    dims, left_cols, cols, keep, left, right, base, out, acc, buffers, l1, l2, l3, inverse, sems, *, scale
+    save = pltpu.make_async_copy(acc.at[pl.ds(0, count)], out, own_sem)
+    save.start()
+
+    def finish(at):
+        half[at] = acc[at].astype(half.dtype)
+
+    each_block(count, finish)
+    save.wait()
+
+
+def cube_here_kernel(
+    dims, left_cols, cols, keep, left, right, base, out, acc, buffers, l1, l2, l3, inverse, sems, own_sem
 ):
-    sub_rows, slots, keeps = dims
-    count = sub_rows * keeps
-    acc[...] = jnp.zeros_like(acc)
+    count = dims[0] * dims[2]
+    load = pltpu.make_async_copy(base, acc.at[pl.ds(0, count)], own_sem)
+    load.start()
     found = (l1, l2, l3)
-    total = list_products(
-        left_cols, left.shape[0], left.shape[0] // sub_rows, cols, slots, keep, keeps, inverse, sub_rows, found
-    )
+    total = listed(dims, left_cols, cols, keep, left, found, inverse)
+    load.wait()
+
+    def begin(at):
+        acc[at] = -1.5 * acc[at]
+
+    each_block(count, begin)
     multiply(total, lambda at: left[at], right, acc, count, found, buffers, sems)
-
-    def finish(at, carry):
-        out[at] = (scale * base[at] - 2.0 * acc[at]).astype(out.dtype)
-        return carry
-
-    lax.fori_loop(0, count, finish, 0)
-
-
-def products(kernel, outs, dims, left_cols, cols, keep, left, right, extra, width, name):
+    save = pltpu.make_async_copy(acc.at[pl.ds(0, count)], out, own_sem)
+    save.start()
+    save.wait()
+
+
+def cube_there_kernel(
+    dims, first, left_cols, cols, keep, left, right, base, *rest
+):
+    out, acc, buffers, l1, l2, l3, inverse, sems, own_sem, done = rest[-10:]
+    count = dims[0] * dims[2]
+    load = pltpu.make_async_copy(base, acc.at[pl.ds(0, count)], own_sem)
+    load.start()
+    found = (l1, l2, l3)
+    total = listed(dims, left_cols, cols, keep, left, found, inverse)
+    load.wait()
+    multiply(total, lambda at: left[at], right, acc, count, found, buffers, sems)
+
+    def finish(at):
+        done[at] = (-2.0 * acc[at]).astype(done.dtype)
+
+    each_block(count, finish)
+    save = pltpu.make_async_copy(done, out.at[pl.ds(first, count)], own_sem)
+    save.start()
+    save.wait()
+
+
+def products(kernel, outs, dims, left_cols, cols, keep, left, right, extra, width, name, more=(), alias=None):
     sub_rows, slots, keeps = dims
     block = left.shape[1:]
     count = sub_rows * keeps
@@ -382,10 +424,10 @@
     hbm = pl.BlockSpec(memory_space=pltpu.HBM)
     scalars = pltpu.SMEM((entries,), jnp.int32)
     return pl.pallas_call(
-        functools.partial(kernel, dims),
-        out_shape=tuple(jax.ShapeDtypeStruct((count,) + block, t) for t in outs),
-        in_specs=[smem] * 3 + [vmem, hbm] + [vmem] * len(extra),
-        out_specs=tuple(vmem for _ in outs),
+        kernel,
+        out_shape=tuple(jax.ShapeDtypeStruct((n,) + block, t) for n, t, place in outs),
+        in_specs=[smem] * 3 + [vmem, hbm] + [hbm] * len(extra),
+        out_specs=tuple({"vmem": vmem, "hbm": hbm}[place] for n, t, place in outs),
         scratch_shapes=[
             pltpu.VMEM((count + 1,) + block, jnp.float32),
             pltpu.VMEM((DEPTH,) + block, right.dtype),
@@ -394,10 +436,13 @@
             scalars,
             pltpu.SMEM((sub_rows * width,), jnp.int32),
             pltpu.SemaphoreType.DMA((DEPTH,)),
+            pltpu.SemaphoreType.DMA,
+            *more,
         ],
+        input_output_aliases={} if alias is None else {alias: 0},
         compiler_params=pltpu.CompilerParams(vmem_limit_bytes=48 * 1024 * 1024),
         cost_estimate=pl.CostEstimate(
-            flops=2 * 2 * count * 128**3, bytes_accessed=30_000_000, transcendentals=0
+            flops=2 * 2 * count * 128**3, bytes_accessed=15_000_000, transcendentals=0
         ),
         name=name,
     )(left_cols, cols, keep, left, right, *extra)
@@ -411,7 +456,6 @@
     keeps = keep_cols.shape[1]
     sub_rows = rows // lax.axis_size("layer")
     width = n_row * rows
-    dims = (sub_rows, slots, keeps)
 
     unused = jnp.zeros((rows, LANES - slots - keeps), jnp.int32)
     meta = jnp.concatenate([p_cols, keep_cols, unused], axis=1)
@@ -423,51 +467,70 @@
     right = full.reshape((width * slots,) + block)
     cols = table[:, :, :slots].reshape(-1)
     meta_here, meta_there = own(meta), own(other_meta)
-    keep_here = meta_here[:, slots : slots + keeps].reshape(-1)
-    keep_there = meta_there[:, slots : slots + keeps].reshape(-1)
-    left = jnp.concatenate([own(p_blocks), other_blocks], axis=1).reshape((-1,) + block)
-    left_cols = jnp.concatenate([meta_here[:, :slots], meta_there[:, :slots]], axis=1).reshape(-1)
-
-    square, half = products(
-        square_kernel,
-        (jnp.float32, jnp.bfloat16),
-        dims,
-        left_cols,
-        cols,
-        keep_here,
-        left,
-        right,
-        (),
-        width,
-        "square",
-    )
-    half_there = lax.ppermute(half, "col", [(0, 1), (1, 0)])
-    (partial,) = products(
-        functools.partial(cube_kernel, scale=3.0),
-        (jnp.float32,),
-        dims,
-        keep_here,
-        cols,
-        keep_here,
-        half,
-        right,
-        (square,),
-        width,
-        "cube_here",
-    )
-    (result,) = products(
-        functools.partial(cube_kernel, scale=1.0),
-        (jnp.bfloat16,),
-        dims,
-        keep_there,
-        cols,
-        keep_here,
-        half_there,
-        right,
-        (partial,),
-        width,
-        "cube_there",
-    )
+    blocks_here = own(p_blocks)
+    lots = 2 if sub_rows % 2 == 0 else 1
+    lot = sub_rows // lots
+    dims = (lot, slots, keeps)
+    count = lot * keeps
+    f32, bf16 = jnp.float32, jnp.bfloat16
+    state = []
+    for at in range(lots):
+        here = meta_here[at * lot : (at + 1) * lot]
+        there = meta_there[at * lot : (at + 1) * lot]
+        keep_here = here[:, slots : slots + keeps].reshape(-1)
+        keep_there = there[:, slots : slots + keeps].reshape(-1)
+        left = jnp.concatenate(
+            [blocks_here[at * lot : (at + 1) * lot], other_blocks[at * lot : (at + 1) * lot]], axis=1
+        ).reshape((-1,) + block)
+        left_cols = jnp.concatenate([here[:, :slots], there[:, :slots]], axis=1).reshape(-1)
+        square, half = products(
+            functools.partial(square_kernel, dims),
+            ((count, f32, "hbm"), (count, bf16, "vmem")),
+            dims,
+            left_cols,
+            cols,
+            keep_here,
+            left,
+            right,
+            (),
+            width,
+            f"square_{at}",
+        )
+        half_there = lax.ppermute(half, "col", [(0, 1), (1, 0)])
+        state.append((keep_here, keep_there, square, half, half_there))
+    partials = []
+    for at, (keep_here, keep_there, square, half, half_there) in enumerate(state):
+        (partial,) = products(
+            functools.partial(cube_here_kernel, dims),
+            ((count, f32, "hbm"),),
+            dims,
+            keep_here,
+            cols,
+            keep_here,
+            half,
+            right,
+            (square,),
+            width,
+            f"cube_here_{at}",
+        )
+        partials.append(partial)
+    result = None
+    for at, (keep_here, keep_there, square, half, half_there) in enumerate(state):
+        (result,) = products(
+            functools.partial(cube_there_kernel, dims, at * count),
+            ((lots * count, bf16, "hbm"),),
+            dims,
+            keep_there,
+            cols,
+            keep_here,
+            half_there,
+            right,
+            (partials[at],) + (() if at == 0 else (result,)),
+            width,
+            f"cube_there_{at}",
+            (pltpu.VMEM((count,) + block, bf16),),
+            None if at == 0 else 6,
+        )
     return result.reshape((sub_rows, keeps) + block)
 
 

time: 237 us -> 210 us (0.89)
  Pallas kernels: 178 us -> 161 us
  waiting for transfers between devices: 48.8 us -> 32.7 us
  local copies, waits for them, and re-layouts: 4.35 us -> 8.72 us
    ppermute x1 -> x2, waiting for transfers between devices: 48.8 us -> 32.7 us  [shards(): half_there = lax.ppermute(half, 'col', [(0, 1), (1, 0)])]
    pallas_call x1, Pallas kernels: 123 us -> 114 us  [gather(): pl.pallas_call(functools.partial(gather_kernel, n_row, lines), out_shape=...]
    pallas_call x3 -> x6, Pallas kernels: 54.2 us -> 47.1 us  [products(): pl.pallas_call(kernel, out_shape=tuple((jax.ShapeDtypeStruct((n,) + block...]
    unnamed x5 -> x15, local copies, waits for them, and re-layouts: 0.77 us -> 4.39 us
    slice x2 -> x6, local copies, waits for them, and re-layouts: 0.14 us -> 2.84 us  [the longest x1 1.53 us: shards(): other_blocks[at * lot:(at + 1) * lot]]
  transfers between devices with their start and end apart: 1 -> 2, of which waited for: 1 -> 2; matrix products, arithmetic and copies ran while one was open for 0% -> 0% of each run, Pallas kernels for 9% -> 16%
where the time goes in v2:
time: 210 us; the launch traced here: 207 us
  Pallas kernels  161 us (77%)
  waiting for transfers between devices  32.7 us (16%)
  local copies, waits for them, and re-layouts  8.72 us (4%)
  starting transfers between devices  2.62 us (1%)
    pallas_call x1, Pallas kernels, gather(): pl.pallas_call(functools.partial(gather_kernel, n_row, lines), out_shape=...  114 us
    pallas_call x6, Pallas kernels, products(): pl.pallas_call(kernel, out_shape=tuple((jax.ShapeDtypeStruct((n,) + block...  47.1 us
    ppermute x2, waiting for transfers between devices, shards(): half_there = lax.ppermute(half, 'col', [(0, 1), (1, 0)])  32.7 us
    unnamed x15, local copies, waits for them, and re-layouts  4.39 us
  transfers between devices with their start and end apart: 2, of which 2 were waited for; matrix products, arithmetic and copies ran while one was open for 0% of the time, Pallas kernels for 16%

profile of v2, /device:TPU:0, one launch (start us, length us, event | category | flops | bytes accessed | tf_op | source)
XLA Modules:
  0.0 207.1 jit_solution(7340603323085896512)
XLA Ops:
  0.0 0.0 copy-start.2
  0.0 0.1 pad.10.clone
  0.1 0.9 copy.6
  1.0 1.4 add_add_fusion.meta_ref
  2.4 0.0 copy-start.6
  2.4 114.0 %gather.1 = (bf16[8,16,5,128,128]{4,3,2,1,0:T(8,128)(2,1)}, s32[8,16,128]{2,1,0:T(8,128)}, bf16[8,5,128,128]{3,2,1,0:T(8,128)(2,1)}, s32[16,128]{1,0:T(8,128)}) custom-call(bf16[16,5,128,128]{3,2,1,0:T(8,128)(2,1)} %blocks_ref.1, s32[16,128]{1,0:T(8,128)} %add_add_fusion.meta_ref), custom_call_target="tpu_custom_call" | custom-call | tf_op jit(solution)/shard_map/gather/pallas_call | solution.py:229
  116.4 0.0 copy-start.5
  116.4 0.0 copy-done.6
  116.4 0.7 constant_dynamic-slice_fusion.2
  117.2 0.1 fusion.3
  117.2 0.0 copy-done.2
  117.2 1.2 constant_dynamic-slice_fusion.1
  118.4 0.0 copy-done.5
  118.4 0.2 reshape.34.cols
  118.6 0.1 reshape.40.keep.left_cols
  118.7 0.1 pad_add_fusion.1
  118.8 0.1 reshape.41.left_cols
  118.8 0.0 copy-start.3
  118.9 0.0 copy-start.4
  118.9 1.5 fusion
  120.4 0.0 copy-done.3
  120.4 0.1 copy-done.4
  120.5 0.2 pad_maximum_fusion
  120.8 7.1 %square_0.1 = (f32[48,128,128]{2,1,0:T(8,128)S(1)}, bf16[48,128,128]{2,1,0:T(8,128)(2,1)S(1)}) custom-call(s32[40]{0:T(128)S(1)} %reshape.41.left_cols, s32[640]{0:T(1024)S(1)} %reshape.34.cols, s32[48]{0:T(128)S(1)} %reshape.40.keep.left_cols, bf16[40,128,128]{2,1,0:T(8,128)(2,1)S(1)} %bitcast.6, bf16[640,128,128]{2,1,0:T(8,128)(2,1)} %bitcast.7), custom_call_target="tpu_custom_call" | custom-call | flops 402653184 | bytes 15000000 | tf_op jit(solution)/shard_map/square_0/pallas_call | solution.py:426
  127.9 0.0 copy-start
  127.9 1.7 copy-done
  129.5 2.4 %collective-permute-start.1 = (bf16[48,128,128]{2,1,0:T(8,128)(2,1)S(1)}, bf16[48,128,128]{2,1,0:T(8,128)(2,1)}, u32[]{:S(2)}, u32[]{:S(2)}) collective-permute-start(bf16[48,128,128]{2,1,0:T(8,128)(2,1)S(1)} %get-tuple-element.19.left), channel_id=1, source_target_pairs={{0,2},{2,0},{1,3},{3,1},{4,6},{6,4},{5,7},{7,5},{8,10},{10,8},{9,1... | collective-permute-start | bytes 4718600 | tf_op jit(solution)/shard_map/ppermute | solution.py:499
  131.9 0.1 reshape.35.keep.left_cols
  132.0 0.1 pad_add_fusion
  132.1 0.1 reshape.36.left_cols
  132.2 8.7 %square_1.1 = (f32[48,128,128]{2,1,0:T(8,128)S(1)}, bf16[48,128,128]{2,1,0:T(8,128)(2,1)}) custom-call(s32[40]{0:T(128)S(1)} %reshape.36.left_cols, s32[640]{0:T(1024)S(1)} %reshape.34.cols, s32[48]{0:T(128)S(1)} %reshape.35.keep.left_cols, bf16[40,128,128]{2,1,0:T(8,128)(2,1)S(1)} %bitcast.5, bf16[640,128,128]{2,1,0:T(8,128)(2,1)} %bitcast.8), custom_call_target="tpu_custom_call" | custom-call | flops 402653184 | bytes 15000000 | tf_op jit(solution)/shard_map/square_1/pallas_call | solution.py:426
  140.8 0.0 copy-start.1
  140.9 1.7 copy-done.1
  142.5 0.2 collective-permute-start
  142.7 0.1 fusion.4
  142.8 0.1 reshape.39.left_cols
  142.9 0.1 reshape.33.left_cols
  143.0 7.4 %cube_here_0.1.base = f32[48,128,128]{2,1,0:T(8,128)S(1)} custom-call(s32[48]{0:T(128)S(1)} %reshape.40.keep.left_cols, s32[640]{0:T(1024)S(1)} %reshape.34.cols, s32[48]{0:T(128)S(1)} %reshape.40.keep.left_cols, bf16[48,128,128]{2,1,0:T(8,128)(2,1)S(1)} %get-tuple-element.19.left, bf16[640,128,128]{2,1,0:T(8,128)(2,1)} %bitcast.9, f32[48,128,128]{2,1,0:T(8,128)} %copy-done), custom_call_target="tpu_custom_call" | custom-call | flops 402653184 | bytes 15000000 | tf_op jit(solution)/shard_map/cube_here_0/pallas_call | solution.py:426
  150.4 9.2 %cube_here_1.1.base = f32[48,128,128]{2,1,0:T(8,128)S(1)} custom-call(s32[48]{0:T(128)S(1)} %reshape.35.keep.left_cols, s32[640]{0:T(1024)S(1)} %reshape.34.cols, s32[48]{0:T(128)S(1)} %reshape.35.keep.left_cols, bf16[48,128,128]{2,1,0:T(8,128)(2,1)} %get-tuple-element.17.left, bf16[640,128,128]{2,1,0:T(8,128)(2,1)} %bitcast.10, f32[48,128,128]{2,1,0:T(8,128)} %copy-done.1), custom_call_target="tpu_custom_call" | custom-call | flops 402653184 | bytes 15000000 | tf_op jit(solution)/shard_map/cube_here_1/pallas_call | solution.py:426
  159.6 7.6 %collective-permute-done.1.left = bf16[48,128,128]{2,1,0:T(8,128)(2,1)} collective-permute-done((bf16[48,128,128]{2,1,0:T(8,128)(2,1)S(1)}, bf16[48,128,128]{2,1,0:T(8,128)(2,1)}, u32[]{:S(2)}, u32[]{:S(2)}) %collective-permute-start.1) | collective-permute-done | bytes 1572896 | tf_op jit(solution)/shard_map/ppermute | solution.py:499
  167.2 8.0 %cube_there_0.1.rest_0_ = bf16[96,128,128]{2,1,0:T(8,128)(2,1)} custom-call(s32[48]{0:T(128)S(1)} %reshape.39.left_cols, s32[640]{0:T(1024)S(1)} %reshape.34.cols, s32[48]{0:T(128)S(1)} %reshape.40.keep.left_cols, bf16[48,128,128]{2,1,0:T(8,128)(2,1)} %collective-permute-done.1.left, bf16[640,128,128]{2,1,0:T(8,128)(2,1)} %bitcast.11, ...), custom_call_target="tpu_custom_call" | custom-call | flops 402653184 | bytes 15000000 | tf_op jit(solution)/shard_map/cube_there_0/pallas_call | solution.py:426
  175.2 25.0 %collective-permute-done.left = bf16[48,128,128]{2,1,0:T(8,128)(2,1)S(1)} collective-permute-done((bf16[48,128,128]{2,1,0:T(8,128)(2,1)}, bf16[48,128,128]{2,1,0:T(8,128)(2,1)S(1)}, u32[]{:S(2)}, u32[]{:S(2)}) %collective-permute-start) | collective-permute-done | bytes 1572896 | tf_op jit(solution)/shard_map/ppermute | solution.py:499
  200.3 6.8 %cube_there_1.1 = bf16[96,128,128]{2,1,0:T(8,128)(2,1)} custom-call(s32[48]{0:T(128)S(1)} %reshape.33.left_cols, s32[640]{0:T(1024)S(1)} %reshape.34.cols, s32[48]{0:T(128)S(1)} %reshape.35.keep.left_cols, bf16[48,128,128]{2,1,0:T(8,128)(2,1)S(1)} %collective-permute-done.left, bf16[640,128,128]{2,1,0:T(8,128)(2,1)} %bitcast.12, ...), custom_call_target="tpu_custom_call", output_to_operand_aliasing={{}: (6, {})} | custom-call | flops 402653184 | bytes 15000000 | tf_op jit(solution)/shard_map/cube_there_1/pallas_call | solution.py:426
  (3 shorter events, 0.0 us)
Async XLA Ops:
  0.0 117.2 %copy-start.2 = (bf16[16,5,128,128]{3,2,1,0:T(8,128)(2,1)S(1)}, bf16[16,5,128,128]{3,2,1,0:T(8,128)(2,1)}, u32[]{:S(2)}) copy-start(bf16[16,5,128,128]{3,2,1,0:T(8,128)(2,1)} %blocks_ref.1) | copy-start | bytes 7864324
  2.4 114.1 %copy-start.6 = (s32[16,128]{1,0:T(8,128)S(1)}, s32[16,128]{1,0:T(8,128)}, u32[]{:S(2)}) copy-start(s32[16,128]{1,0:T(8,128)} %add_add_fusion.meta_ref) | copy-start | bytes 24580
  116.4 2.0 copy-start.5
  118.8 1.5 copy-start.3
  118.9 1.7 copy-start.4
  127.9 1.7 copy-start
  129.5 37.7 %collective-permute-start.1 = (bf16[48,128,128]{2,1,0:T(8,128)(2,1)S(1)}, bf16[48,128,128]{2,1,0:T(8,128)(2,1)}, u32[]{:S(2)}, u32[]{:S(2)}) collective-permute-start(bf16[48,128,128]{2,1,0:T(8,128)(2,1)S(1)} %get-tuple-element.19.left), channel_id=1, source_target_pairs={{0,2},{2,0},{1,3},{3,1},{4,6},{6,4},{5,7},{7,5},{8,10},{10,8},{9,1... | collective-permute-start | bytes 4718600 | tf_op jit(solution)/shard_map/ppermute | solution.py:499
  140.8 1.7 copy-start.1
  142.5 57.8 %collective-permute-start = (bf16[48,128,128]{2,1,0:T(8,128)(2,1)}, bf16[48,128,128]{2,1,0:T(8,128)(2,1)S(1)}, u32[]{:S(2)}, u32[]{:S(2)}) collective-permute-start(bf16[48,128,128]{2,1,0:T(8,128)(2,1)} %get-tuple-element.17.left), channel_id=1, source_target_pairs={{0,2},{2,0},{1,3},{3,1},{4,6},{6,4},{5,7},{7,5},{8,10},{10,8},{9,1... | collective-permute-start | bytes 4718600 | tf_op jit(solution)/shard_map/ppermute | solution.py:499

commit v3 on v2

--- a/solution.py
+++ b/solution.py
@@ -219,9 +219,7 @@
 
 def gather(blocks, meta, n_row):
     rows, slots = blocks.shape[:2]
-    turn = slots - max(slots // 5, 1)
-    middle = turn // 2
-    lines = ((0, middle), (middle, turn), (turn, slots))
+    lines = tuple((at, at + 1) for at in range(slots))
     parts = len(lines)
     length = n_row // 2
     anywhere = pl.BlockSpec(memory_space=pl.ANY)
@@ -356,20 +354,39 @@
 
 
 def square_kernel(
-    dims, left_cols, cols, keep, left, right, out, half, acc, buffers, l1, l2, l3, inverse, sems, own_sem
+    dims, first, left_cols, cols, keep, here, there, right, *rest
 ):
-    count = dims[0] * dims[2]
+    out, half, acc, buffers, l1, l2, l3, inverse, sems, own_sem, left, rounded, left_sems, half_sem = rest[-14:]
+    sub_rows, slots, keeps = dims
+    count = sub_rows * keeps
+    layer = lax.axis_index("layer")
+    start = layer * there.shape[0] + first
+    loads = []
+    for row in range(sub_rows):
+        for at, blocks in enumerate((here.at[start + row], there.at[first + row])):
+            loads.append(
+                pltpu.make_async_copy(
+                    blocks, left.at[pl.ds((2 * row + at) * slots, slots)], left_sems.at[2 * row + at]
+                )
+            )
+    for load in loads:
+        load.start()
     acc[...] = jnp.zeros_like(acc)
     found = (l1, l2, l3)
     total = listed(dims, left_cols, cols, keep, left, found, inverse)
+    for load in loads:
+        load.wait()
     multiply(total, lambda at: left[at], right, acc, count, found, buffers, sems)
     save = pltpu.make_async_copy(acc.at[pl.ds(0, count)], out, own_sem)
     save.start()
 
     def finish(at):
-        half[at] = acc[at].astype(half.dtype)
+        rounded[at] = acc[at].astype(rounded.dtype)
 
     each_block(count, finish)
+    send = pltpu.make_async_copy(rounded, half, half_sem)
+    send.start()
+    send.wait()
     save.wait()
 
 
@@ -416,9 +433,9 @@
 
 def products(kernel, outs, dims, left_cols, cols, keep, left, right, extra, width, name, more=(), alias=None):
     sub_rows, slots, keeps = dims
-    block = left.shape[1:]
+    block = right.shape[1:]
     count = sub_rows * keeps
-    entries = left.shape[0] * slots + GROUP
+    entries = left_cols.shape[0] * slots + GROUP
     smem = pl.BlockSpec(memory_space=pltpu.SMEM)
     vmem = pl.BlockSpec(memory_space=pltpu.VMEM)
     hbm = pl.BlockSpec(memory_space=pltpu.HBM)
@@ -426,7 +443,7 @@
     return pl.pallas_call(
         kernel,
         out_shape=tuple(jax.ShapeDtypeStruct((n,) + block, t) for n, t, place in outs),
-        in_specs=[smem] * 3 + [vmem, hbm] + [hbm] * len(extra),
+        in_specs=[smem] * 3 + [vmem if len(left) == 1 else hbm] * len(left) + [hbm] * (1 + len(extra)),
         out_specs=tuple({"vmem": vmem, "hbm": hbm}[place] for n, t, place in outs),
         scratch_shapes=[
             pltpu.VMEM((count + 1,) + block, jnp.float32),
@@ -445,7 +462,7 @@
             flops=2 * 2 * count * 128**3, bytes_accessed=15_000_000, transcendentals=0
         ),
         name=name,
-    )(left_cols, cols, keep, left, right, *extra)
+    )(left_cols, cols, keep, *left, right, *extra)
 
 
 def shards(p_blocks, p_cols, keep_cols):
@@ -467,69 +484,72 @@
     right = full.reshape((width * slots,) + block)
     cols = table[:, :, :slots].reshape(-1)
     meta_here, meta_there = own(meta), own(other_meta)
-    blocks_here = own(p_blocks)
-    lots = 2 if sub_rows % 2 == 0 else 1
-    lot = sub_rows // lots
-    dims = (lot, slots, keeps)
-    count = lot * keeps
+    tail = max(sub_rows // 8, 1)
+    middle = (sub_rows - 2 * tail) // 2
+    cuts = (0, tail, tail + middle, sub_rows - tail, sub_rows)
+    lots = [(lo, hi) for lo, hi in zip(cuts[:-1], cuts[1:]) if hi > lo]
     f32, bf16 = jnp.float32, jnp.bfloat16
     state = []
-    for at in range(lots):
-        here = meta_here[at * lot : (at + 1) * lot]
-        there = meta_there[at * lot : (at + 1) * lot]
+    for lo, hi in lots:
+        dims = (hi - lo, slots, keeps)
+        count = (hi - lo) * keeps
+        here, there = meta_here[lo:hi], meta_there[lo:hi]
         keep_here = here[:, slots : slots + keeps].reshape(-1)
         keep_there = there[:, slots : slots + keeps].reshape(-1)
-        left = jnp.concatenate(
-            [blocks_here[at * lot : (at + 1) * lot], other_blocks[at * lot : (at + 1) * lot]], axis=1
-        ).reshape((-1,) + block)
         left_cols = jnp.concatenate([here[:, :slots], there[:, :slots]], axis=1).reshape(-1)
         square, half = products(
-            functools.partial(square_kernel, dims),
-            ((count, f32, "hbm"), (count, bf16, "vmem")),
+            functools.partial(square_kernel, dims, lo),
+            ((count, f32, "hbm"), (count, bf16, "hbm")),
             dims,
             left_cols,
             cols,
             keep_here,
-            left,
+            (p_blocks, other_blocks),
             right,
-            (),
+            tuple(entry[4] for entry in state[-1:]),
             width,
-            f"square_{at}",
+            f"square_{lo}",
+            (
+                pltpu.VMEM(((hi - lo) * 2 * slots,) + block, bf16),
+                pltpu.VMEM((count,) + block, bf16),
+                pltpu.SemaphoreType.DMA(((hi - lo) * 2,)),
+                pltpu.SemaphoreType.DMA,
+            ),
         )
         half_there = lax.ppermute(half, "col", [(0, 1), (1, 0)])
-        state.append((keep_here, keep_there, square, half, half_there))
+        state.append((lo, dims, keep_here, keep_there, square, half, half_there))
     partials = []
-    for at, (keep_here, keep_there, square, half, half_there) in enumerate(state):
+    for lo, dims, keep_here, keep_there, square, half, half_there in state:
         (partial,) = products(
             functools.partial(cube_here_kernel, dims),
-            ((count, f32, "hbm"),),
+            ((half.shape[0], f32, "hbm"),),
             dims,
             keep_here,
             cols,
             keep_here,
-            half,
+            (half,),
             right,
             (square,),
             width,
-            f"cube_here_{at}",
+            f"cube_here_{lo}",
         )
         partials.append(partial)
     result = None
-    for at, (keep_here, keep_there, square, half, half_there) in enumerate(state):
+    for partial, (lo, dims, keep_here, keep_there, square, half, half_there) in zip(partials, state):
         (result,) = products(
-            functools.partial(cube_there_kernel, dims, at * count),
-            ((lots * count, bf16, "hbm"),),
+            functools.partial(cube_there_kernel, dims, lo * keeps),
+            ((sub_rows * keeps, bf16, "hbm"),),
             dims,
             keep_there,
             cols,
             keep_here,
-            half_there,
+            (half_there,),
             right,
-            (partials[at],) + (() if at == 0 else (result,)),
+            (partial,) + (() if result is None else (result,)),
             width,
-            f"cube_there_{at}",
-            (pltpu.VMEM((count,) + block, bf16),),
-            None if at == 0 else 6,
+            f"cube_there_{lo}",
+            (pltpu.VMEM(half.shape, bf16),),
+            None if result is None else 6,
         )
     return result.reshape((sub_rows, keeps) + block)
 

time: 210 us -> 222 us (1.057)
  Pallas kernels: 161 us -> 185 us
  waiting for transfers between devices: 32.7 us -> 20.5 us
    pallas_call x6 -> x12, Pallas kernels: 47.1 us -> 70.1 us  [products(): pl.pallas_call(kernel, out_shape=tuple((jax.ShapeDtypeStruct((n,) + block...]
    ppermute x2 -> x4, waiting for transfers between devices: 32.7 us -> 20.5 us  [shards(): half_there = lax.ppermute(half, 'col', [(0, 1), (1, 0)])]
    slice x2 -> x0, local copies, waits for them, and re-layouts: 2.69 us -> none  [the longest x1 1.53 us: shards(): other_blocks[at * lot:(at + 1) * lot]]
    unnamed x15 -> x21, local copies, waits for them, and re-layouts: 4.39 us -> 4.54 us
  transfers between devices with their start and end apart: 2 -> 4, of which waited for: 2 -> 1; matrix products, arithmetic and copies ran while one was open for 0% -> 0% of each run, Pallas kernels for 16% -> 25%
where the time goes in v3:
time: 222 us; the launch traced here: 218 us
  Pallas kernels  185 us (83%)
  waiting for transfers between devices  20.5 us (9%)
  local copies, waits for them, and re-layouts  7.15 us (3%)
  starting transfers between devices  3.82 us (2%)
    pallas_call x1, Pallas kernels, gather(): pl.pallas_call(functools.partial(gather_kernel, n_row, lines), out_shape=...  115 us
    pallas_call x12, Pallas kernels, products(): pl.pallas_call(kernel, out_shape=tuple((jax.ShapeDtypeStruct((n,) + block...  70.1 us
    ppermute x4, waiting for transfers between devices, shards(): half_there = lax.ppermute(half, 'col', [(0, 1), (1, 0)])  20.5 us
    unnamed x21, local copies, waits for them, and re-layouts  4.54 us
  transfers between devices with their start and end apart: 4, of which 1 were waited for; matrix products, arithmetic and copies ran while one was open for 0% of the time, Pallas kernels for 25%

profile of v3, /device:TPU:0, one launch (start us, length us, event | category | flops | bytes accessed | tf_op | source)
XLA Modules:
  0.0 218.3 jit_solution(15196474914419318161)
XLA Ops:
  0.0 0.0 copy-start
  0.0 0.1 pad.10.clone
  0.1 0.9 copy.8
  1.0 1.4 add_add_fusion.meta_ref
  2.4 0.0 copy-start.9
  2.4 114.9 %gather.1 = (bf16[8,16,5,128,128]{4,3,2,1,0:T(8,128)(2,1)}, s32[8,16,128]{2,1,0:T(8,128)}, bf16[8,5,128,128]{3,2,1,0:T(8,128)(2,1)}, s32[16,128]{1,0:T(8,128)}) custom-call(bf16[16,5,128,128]{3,2,1,0:T(8,128)(2,1)} %here.7, s32[16,128]{1,0:T(8,128)} %add_add_fusion.meta_ref), custom_call_target="tpu_custom_call" | custom-call | tf_op jit(solution)/shard_map/gather/pallas_call | solution.py:227
  117.3 0.0 copy-done.9
  117.3 0.7 constant_dynamic-slice_fusion
  118.0 0.1 slice_bitcast_fusion.1
  118.1 0.1 fusion.3
  118.2 1.0 reshape.46.cols
  119.2 0.1 reshape.53.keep.left_cols
  119.3 0.1 pad_add_fusion.1
  119.4 0.1 reshape.52.left_cols
  119.4 0.1 add_bitcast_fusion.1.left_cols
  119.5 0.0 copy-done
  119.5 0.0 copy-start.1
  119.5 1.3 copy-done.1
  120.8 4.7 %square_0.1 = (f32[12,128,128]{2,1,0:T(8,128)S(1)}, bf16[12,128,128]{2,1,0:T(8,128)(2,1)}) custom-call(s32[10]{0:T(128)S(1)} %add_bitcast_fusion.1.left_cols, s32[640]{0:T(1024)S(1)} %reshape.46.cols, s32[12]{0:T(128)S(1)} %get-tuple-element.33.keep.left_cols, bf16[16,5,128,128]{3,2,1,0:T(8,128)(2,1)S(1)} %copy-done, bf16[8,5,128,128]{3,2,1,0:T(8,128)(2,1)S(1)} %copy-done.1, ...), custom_call_target="tpu_custom_call" | custom-call | flops 100663296 | bytes 15000000 | tf_op jit(solution)/shard_map/square_0/pallas_call | solution.py:443
  125.5 0.0 copy-start.2
  125.5 8.1 %square_1.1 = (f32[36,128,128]{2,1,0:T(8,128)S(1)}, bf16[36,128,128]{2,1,0:T(8,128)(2,1)}) custom-call(s32[30]{0:T(128)S(1)} %reshape.52.left_cols, s32[640]{0:T(1024)S(1)} %reshape.46.cols, s32[36]{0:T(128)S(1)} %reshape.53.keep.left_cols, bf16[16,5,128,128]{3,2,1,0:T(8,128)(2,1)} %here.7, bf16[8,5,128,128]{3,2,1,0:T(8,128)(2,1)S(1)} %copy-done.1, ...), custom_call_target="tpu_custom_call" | custom-call | flops 301989888 | bytes 15000000 | tf_op jit(solution)/shard_map/square_1/pallas_call | solution.py:443
  133.6 0.0 copy-start.3
  133.7 1.4 copy-done.3
  135.1 1.0 collective-permute-start.2
  136.1 0.1 reshape.51.keep.left_cols
  136.1 0.1 pad_add_fusion
  136.2 0.1 reshape.50.left_cols
  136.3 0.0 copy-done.2
  136.3 8.2 %square_4.1 = (f32[36,128,128]{2,1,0:T(8,128)S(1)}, bf16[36,128,128]{2,1,0:T(8,128)(2,1)}) custom-call(s32[30]{0:T(128)S(1)} %reshape.50.left_cols, s32[640]{0:T(1024)S(1)} %reshape.46.cols, s32[36]{0:T(128)S(1)} %reshape.51.keep.left_cols, bf16[16,5,128,128]{3,2,1,0:T(8,128)(2,1)} %here.7, bf16[8,5,128,128]{3,2,1,0:T(8,128)(2,1)S(1)} %copy-done.2, ...), custom_call_target="tpu_custom_call" | custom-call | flops 301989888 | bytes 15000000 | tf_op jit(solution)/shard_map/square_4/pallas_call | solution.py:443
  144.5 0.0 copy-start.5
  144.5 1.3 collective-permute-start.1
  145.8 0.8 collective-permute-start.3
  146.6 0.1 add_bitcast_fusion.left_cols
  146.7 4.7 %square_7.1 = (f32[12,128,128]{2,1,0:T(8,128)S(1)}, bf16[12,128,128]{2,1,0:T(8,128)(2,1)}) custom-call(s32[10]{0:T(128)S(1)} %add_bitcast_fusion.left_cols, s32[640]{0:T(1024)S(1)} %reshape.46.cols, s32[12]{0:T(128)S(1)} %get-tuple-element.34.keep.left_cols, bf16[16,5,128,128]{3,2,1,0:T(8,128)(2,1)} %here.7, bf16[8,5,128,128]{3,2,1,0:T(8,128)(2,1)S(1)} %copy-done.2, ...), custom_call_target="tpu_custom_call" | custom-call | flops 100663296 | bytes 15000000 | tf_op jit(solution)/shard_map/square_7/pallas_call | solution.py:443
  151.4 0.0 copy-done.5
  151.4 0.0 copy-start.7
  151.4 0.9 copy-done.7
  152.3 0.7 collective-permute-start
  153.0 0.1 fusion
  153.1 0.1 reshape.57.left_cols
  153.2 0.1 reshape.56.left_cols
  153.2 0.0 copy-start.8
  153.2 4.3 %cube_here_0.1.base = f32[12,128,128]{2,1,0:T(8,128)S(1)} custom-call(s32[12]{0:T(128)S(1)} %get-tuple-element.33.keep.left_cols, s32[640]{0:T(1024)S(1)} %reshape.46.cols, s32[12]{0:T(128)S(1)} %get-tuple-element.33.keep.left_cols, bf16[12,128,128]{2,1,0:T(8,128)(2,1)} %get-tuple-element.28.left, bf16[640,128,128]{2,1,0:T(8,128)(2,1)} %bitcast.19, ...), custom_call_target="tpu_custom_call" | custom-call | flops 100663296 | bytes 15000000 | tf_op jit(solution)/shard_map/cube_here_0/pallas_call | solution.py:443
  157.5 0.0 copy-done.8
  157.5 0.0 copy-start.4
  157.5 4.5 %cube_here_7.1.base = f32[12,128,128]{2,1,0:T(8,128)S(1)} custom-call(s32[12]{0:T(128)S(1)} %get-tuple-element.34.keep.left_cols, s32[640]{0:T(1024)S(1)} %reshape.46.cols, s32[12]{0:T(128)S(1)} %get-tuple-element.34.keep.left_cols, bf16[12,128,128]{2,1,0:T(8,128)(2,1)} %get-tuple-element.24.left, bf16[640,128,128]{2,1,0:T(8,128)(2,1)} %bitcast.20, ...), custom_call_target="tpu_custom_call" | custom-call | flops 100663296 | bytes 15000000 | tf_op jit(solution)/shard_map/cube_here_7/pallas_call | solution.py:443
  162.1 0.0 copy-done.4
  162.1 0.0 copy-start.6
  162.1 7.9 %cube_here_1.1.base = f32[36,128,128]{2,1,0:T(8,128)S(1)} custom-call(s32[36]{0:T(128)S(1)} %reshape.53.keep.left_cols, s32[640]{0:T(1024)S(1)} %reshape.46.cols, s32[36]{0:T(128)S(1)} %reshape.53.keep.left_cols, bf16[36,128,128]{2,1,0:T(8,128)(2,1)} %get-tuple-element.27.left, bf16[640,128,128]{2,1,0:T(8,128)(2,1)} %bitcast.21, f32[36,128,128]{2,1,0:T(8,128)S(1)} %copy-done.4), custom_call_target="tpu_custom_call" | custom-call | flops 301989888 | bytes 15000000 | tf_op jit(solution)/shard_map/cube_here_1/pallas_call | solution.py:443
  170.0 0.0 copy-done.6
  170.0 7.3 %cube_here_4.1.base = f32[36,128,128]{2,1,0:T(8,128)S(1)} custom-call(s32[36]{0:T(128)S(1)} %reshape.51.keep.left_cols, s32[640]{0:T(1024)S(1)} %reshape.46.cols, s32[36]{0:T(128)S(1)} %reshape.51.keep.left_cols, bf16[36,128,128]{2,1,0:T(8,128)(2,1)} %get-tuple-element.26.left, bf16[640,128,128]{2,1,0:T(8,128)(2,1)} %bitcast.22, f32[36,128,128]{2,1,0:T(8,128)S(1)} %copy-done.6), custom_call_target="tpu_custom_call" | custom-call | flops 301989888 | bytes 15000000 | tf_op jit(solution)/shard_map/cube_here_4/pallas_call | solution.py:443
  177.4 0.1 slice_bitcast_fusion
  177.4 20.5 %collective-permute-done.3.left = bf16[12,128,128]{2,1,0:T(8,128)(2,1)} collective-permute-done((bf16[12,128,128]{2,1,0:T(8,128)(2,1)}, bf16[12,128,128]{2,1,0:T(8,128)(2,1)}, u32[]{:S(2)}, u32[]{:S(2)}) %collective-permute-start.3) | collective-permute-done | bytes 393248 | tf_op jit(solution)/shard_map/ppermute | solution.py:519
  197.9 4.2 %cube_there_0.1.rest_0_ = bf16[96,128,128]{2,1,0:T(8,128)(2,1)} custom-call(s32[12]{0:T(128)S(1)} %get-tuple-element.29.left_cols, s32[640]{0:T(1024)S(1)} %reshape.46.cols, s32[12]{0:T(128)S(1)} %get-tuple-element.33.keep.left_cols, bf16[12,128,128]{2,1,0:T(8,128)(2,1)} %collective-permute-done.3.left, bf16[640,128,128]{2,1,0:T(8,128)(2,1)} %bitcast.23, ...), custom_call_target="tpu_custom_call" | custom-call | flops 100663296 | bytes 15000000 | tf_op jit(solution)/shard_map/cube_there_0/pallas_call | solution.py:443
  202.1 0.0 collective-permute-done.2.left
  202.1 5.9 %cube_there_1.1.rest_0_ = bf16[96,128,128]{2,1,0:T(8,128)(2,1)} custom-call(s32[36]{0:T(128)S(1)} %reshape.57.left_cols, s32[640]{0:T(1024)S(1)} %reshape.46.cols, s32[36]{0:T(128)S(1)} %reshape.53.keep.left_cols, bf16[36,128,128]{2,1,0:T(8,128)(2,1)S(1)} %collective-permute-done.2.left, ...), custom_call_target="tpu_custom_call", output_to_operand_aliasing={{}: (6, {})} | custom-call | flops 301989888 | bytes 15000000 | tf_op jit(solution)/shard_map/cube_there_1/pallas_call | solution.py:443
  208.1 0.0 collective-permute-done.1.left
  208.1 6.6 %cube_there_4.1.rest_0_ = bf16[96,128,128]{2,1,0:T(8,128)(2,1)} custom-call(s32[36]{0:T(128)S(1)} %reshape.56.left_cols, s32[640]{0:T(1024)S(1)} %reshape.46.cols, s32[36]{0:T(128)S(1)} %reshape.51.keep.left_cols, bf16[36,128,128]{2,1,0:T(8,128)(2,1)} %collective-permute-done.1.left, ...), custom_call_target="tpu_custom_call", output_to_operand_aliasing={{}: (6, {})} | custom-call | flops 301989888 | bytes 15000000 | tf_op jit(solution)/shard_map/cube_there_4/pallas_call | solution.py:443
  214.7 0.0 collective-permute-done.left
  214.7 3.6 %cube_there_7.1 = bf16[96,128,128]{2,1,0:T(8,128)(2,1)} custom-call(s32[12]{0:T(128)S(1)} %get-tuple-element.30.left_cols, s32[640]{0:T(1024)S(1)} %reshape.46.cols, s32[12]{0:T(128)S(1)} %get-tuple-element.34.keep.left_cols, bf16[12,128,128]{2,1,0:T(8,128)(2,1)S(1)} %collective-permute-done.left, ...), custom_call_target="tpu_custom_call", output_to_operand_aliasing={{}: (6, {})} | custom-call | flops 100663296 | bytes 15000000 | tf_op jit(solution)/shard_map/cube_there_7/pallas_call | solution.py:443
  (5 shorter events, 0.0 us)
Async XLA Ops:
  0.0 119.5 %copy-start = (bf16[16,5,128,128]{3,2,1,0:T(8,128)(2,1)S(1)}, bf16[16,5,128,128]{3,2,1,0:T(8,128)(2,1)}, u32[]{:S(2)}) copy-start(bf16[16,5,128,128]{3,2,1,0:T(8,128)(2,1)} %here.7) | copy-start | bytes 7864324
  2.4 114.9 %copy-start.9 = (s32[16,128]{1,0:T(8,128)S(1)}, s32[16,128]{1,0:T(8,128)}, u32[]{:S(2)}) copy-start(s32[16,128]{1,0:T(8,128)} %add_add_fusion.meta_ref) | copy-start | bytes 24580
  119.5 1.3 copy-start.1
  125.5 10.8 %copy-start.2 = (bf16[8,5,128,128]{3,2,1,0:T(8,128)(2,1)S(1)}, bf16[8,5,128,128]{3,2,1,0:T(8,128)(2,1)}, u32[]{:S(2)}) copy-start(bf16[8,5,128,128]{3,2,1,0:T(8,128)(2,1)} %get-tuple-element.19.there) | copy-start | bytes 3932164
  133.6 1.4 copy-start.3
  135.1 67.1 %collective-permute-start.2 = (bf16[36,128,128]{2,1,0:T(8,128)(2,1)}, bf16[36,128,128]{2,1,0:T(8,128)(2,1)S(1)}, u32[]{:S(2)}, u32[]{:S(2)}) collective-permute-start(bf16[36,128,128]{2,1,0:T(8,128)(2,1)} %get-tuple-element.27.left), channel_id=1, source_target_pairs={{0,2},{2,0},{1,3},{3,1},{4,6},{6,4},{5,7},{7,5},{8,10},{10,8},{9,1... | collective-permute-start | bytes 3538952 | tf_op jit(solution)/shard_map/ppermute | solution.py:519
  144.5 6.9 %copy-start.5 = (f32[36,128,128]{2,1,0:T(8,128)}, f32[36,128,128]{2,1,0:T(8,128)S(1)}, u32[]{:S(2)}) copy-start(f32[36,128,128]{2,1,0:T(8,128)S(1)} %get-tuple-element.23.rest_0_.base) | copy-start | bytes 7077892
  144.5 63.6 %collective-permute-start.1 = (bf16[36,128,128]{2,1,0:T(8,128)(2,1)}, bf16[36,128,128]{2,1,0:T(8,128)(2,1)}, u32[]{:S(2)}, u32[]{:S(2)}) collective-permute-start(bf16[36,128,128]{2,1,0:T(8,128)(2,1)} %get-tuple-element.26.left), channel_id=1, source_target_pairs={{0,2},{2,0},{1,3},{3,1},{4,6},{6,4},{5,7},{7,5},{8,10},{10,8},{9,1... | collective-permute-start | bytes 3538952 | tf_op jit(solution)/shard_map/ppermute | solution.py:519
  145.8 52.1 %collective-permute-start.3 = (bf16[12,128,128]{2,1,0:T(8,128)(2,1)}, bf16[12,128,128]{2,1,0:T(8,128)(2,1)}, u32[]{:S(2)}, u32[]{:S(2)}) collective-permute-start(bf16[12,128,128]{2,1,0:T(8,128)(2,1)} %get-tuple-element.28.left), channel_id=1, source_target_pairs={{0,2},{2,0},{1,3},{3,1},{4,6},{6,4},{5,7},{7,5},{8,10},{10,8},{9,1... | collective-permute-start | bytes 1179656 | tf_op jit(solution)/shard_map/ppermute | solution.py:519
  151.4 0.9 copy-start.7
  152.3 62.4 %collective-permute-start = (bf16[12,128,128]{2,1,0:T(8,128)(2,1)}, bf16[12,128,128]{2,1,0:T(8,128)(2,1)S(1)}, u32[]{:S(2)}, u32[]{:S(2)}) collective-permute-start(bf16[12,128,128]{2,1,0:T(8,128)(2,1)} %get-tuple-element.24.left), channel_id=1, source_target_pairs={{0,2},{2,0},{1,3},{3,1},{4,6},{6,4},{5,7},{7,5},{8,10},{10,8},{9,1... | collective-permute-start | bytes 1179656 | tf_op jit(solution)/shard_map/ppermute | solution.py:519
  153.2 4.3 %copy-start.8 = (f32[12,128,128]{2,1,0:T(8,128)S(1)}, f32[12,128,128]{2,1,0:T(8,128)}, u32[]{:S(2)}) copy-start(f32[12,128,128]{2,1,0:T(8,128)} %copy-done.7) | copy-start | bytes 2359300
  157.5 4.6 %copy-start.4 = (f32[36,128,128]{2,1,0:T(8,128)S(1)}, f32[36,128,128]{2,1,0:T(8,128)}, u32[]{:S(2)}) copy-start(f32[36,128,128]{2,1,0:T(8,128)} %copy-done.3) | copy-start | bytes 7077892
  162.1 7.9 %copy-start.6 = (f32[36,128,128]{2,1,0:T(8,128)S(1)}, f32[36,128,128]{2,1,0:T(8,128)}, u32[]{:S(2)}) copy-start(f32[36,128,128]{2,1,0:T(8,128)} %copy-done.5) | copy-start | bytes 7077892

commit v4 on v3

--- a/solution.py
+++ b/solution.py
@@ -219,7 +219,9 @@
 
 def gather(blocks, meta, n_row):
     rows, slots = blocks.shape[:2]
-    lines = tuple((at, at + 1) for at in range(slots))
+    turn = slots - max(slots // 5, 1)
+    middle = turn // 2
+    lines = ((0, middle), (middle, turn), (turn, slots))
     parts = len(lines)
     length = n_row // 2
     anywhere = pl.BlockSpec(memory_space=pl.ANY)
@@ -391,14 +393,18 @@
 
 
 def cube_here_kernel(
-    dims, left_cols, cols, keep, left, right, base, out, acc, buffers, l1, l2, l3, inverse, sems, own_sem
+    dims, left_cols, cols, keep, blocks, right, base, *rest
 ):
+    out, acc, buffers, l1, l2, l3, inverse, sems, own_sem, left, left_sem = rest[-11:]
     count = dims[0] * dims[2]
+    fetch = pltpu.make_async_copy(blocks, left, left_sem)
+    fetch.start()
     load = pltpu.make_async_copy(base, acc.at[pl.ds(0, count)], own_sem)
     load.start()
     found = (l1, l2, l3)
     total = listed(dims, left_cols, cols, keep, left, found, inverse)
     load.wait()
+    fetch.wait()
 
     def begin(at):
         acc[at] = -1.5 * acc[at]
@@ -411,15 +417,18 @@
 
 
 def cube_there_kernel(
-    dims, first, left_cols, cols, keep, left, right, base, *rest
+    dims, first, left_cols, cols, keep, blocks, right, base, *rest
 ):
-    out, acc, buffers, l1, l2, l3, inverse, sems, own_sem, done = rest[-10:]
+    out, acc, buffers, l1, l2, l3, inverse, sems, own_sem, left, left_sem, done = rest[-12:]
     count = dims[0] * dims[2]
+    fetch = pltpu.make_async_copy(blocks, left, left_sem)
+    fetch.start()
     load = pltpu.make_async_copy(base, acc.at[pl.ds(0, count)], own_sem)
     load.start()
     found = (l1, l2, l3)
     total = listed(dims, left_cols, cols, keep, left, found, inverse)
     load.wait()
+    fetch.wait()
     multiply(total, lambda at: left[at], right, acc, count, found, buffers, sems)
 
     def finish(at):
@@ -443,7 +452,7 @@
     return pl.pallas_call(
         kernel,
         out_shape=tuple(jax.ShapeDtypeStruct((n,) + block, t) for n, t, place in outs),
-        in_specs=[smem] * 3 + [vmem if len(left) == 1 else hbm] * len(left) + [hbm] * (1 + len(extra)),
+        in_specs=[smem] * 3 + [hbm] * (len(left) + 1 + len(extra)),
         out_specs=tuple({"vmem": vmem, "hbm": hbm}[place] for n, t, place in outs),
         scratch_shapes=[
             pltpu.VMEM((count + 1,) + block, jnp.float32),
@@ -457,9 +466,9 @@
             *more,
         ],
         input_output_aliases={} if alias is None else {alias: 0},
-        compiler_params=pltpu.CompilerParams(vmem_limit_bytes=48 * 1024 * 1024),
+        compiler_params=pltpu.CompilerParams(vmem_limit_bytes=64 * 1024 * 1024),
         cost_estimate=pl.CostEstimate(
-            flops=2 * 2 * count * 128**3, bytes_accessed=15_000_000, transcendentals=0
+flops=1000, bytes_accessed=1000, transcendentals=0
         ),
         name=name,
     )(left_cols, cols, keep, *left, right, *extra)
@@ -484,9 +493,9 @@
     right = full.reshape((width * slots,) + block)
     cols = table[:, :, :slots].reshape(-1)
     meta_here, meta_there = own(meta), own(other_meta)
-    tail = max(sub_rows // 8, 1)
+    tail = max(sub_rows // 4, 1)
     middle = (sub_rows - 2 * tail) // 2
-    cuts = (0, tail, tail + middle, sub_rows - tail, sub_rows)
+    cuts = (0, tail, sub_rows - tail, sub_rows)
     lots = [(lo, hi) for lo, hi in zip(cuts[:-1], cuts[1:]) if hi > lo]
     f32, bf16 = jnp.float32, jnp.bfloat16
     state = []
@@ -506,7 +515,7 @@
             keep_here,
             (p_blocks, other_blocks),
             right,
-            tuple(entry[4] for entry in state[-1:]),
+            tuple(entry[4] for entry in state[-1:]) + tuple(entry[-1] for entry in state[:-1]),
             width,
             f"square_{lo}",
             (
@@ -532,6 +541,7 @@
             (square,),
             width,
             f"cube_here_{lo}",
+            (pltpu.VMEM(half.shape, bf16), pltpu.SemaphoreType.DMA),
         )
         partials.append(partial)
     result = None
@@ -548,7 +558,7 @@
             (partial,) + (() if result is None else (result,)),
             width,
             f"cube_there_{lo}",
-            (pltpu.VMEM(half.shape, bf16),),
+            (pltpu.VMEM(half.shape, bf16), pltpu.SemaphoreType.DMA, pltpu.VMEM(half.shape, bf16)),
             None if result is None else 6,
         )
     return result.reshape((sub_rows, keeps) + block)

time: 222 us -> 207 us (0.932)
  waiting for transfers between devices: 20.5 us -> 5.48 us
  Pallas kernels: 185 us -> 176 us
  local copies, waits for them, and re-layouts: 7.15 us -> 14.6 us
    ppermute x4 -> x3, waiting for transfers between devices: 20.5 us -> 5.48 us  [shards(): half_there = lax.ppermute(half, 'col', [(0, 1), (1, 0)])]
    pallas_call x12 -> x9, Pallas kernels: 70.1 us -> 62.1 us  [products(): pl.pallas_call(kernel, out_shape=tuple((jax.ShapeDtypeStruct((n,) + block...]
    unnamed x21 -> x7, local copies, waits for them, and re-layouts: 4.54 us -> 0.77 us
    ppermute x4 -> x3, starting transfers between devices: 3.82 us -> 5 us  [shards(): half_there = lax.ppermute(half, 'col', [(0, 1), (1, 0)])]
  transfers between devices with their start and end apart: 4 -> 3, of which waited for: 1 -> 2; matrix products, arithmetic and copies ran while one was open for 0% -> 5% of each run, Pallas kernels for 25% -> 25%
where the time goes in v4:
time: 207 us; the launch traced here: 204 us
  Pallas kernels  176 us (85%)
  local copies, waits for them, and re-layouts  14.6 us (7%)
  waiting for transfers between devices  5.48 us (3%)
  starting transfers between devices  5 us (2%)
  other arithmetic  2.28 us (1%)
    pallas_call x1, Pallas kernels, gather(): pl.pallas_call(functools.partial(gather_kernel, n_row, lines), out_shape=...  114 us
    pallas_call x9, Pallas kernels, products(): pl.pallas_call(kernel, out_shape=tuple((jax.ShapeDtypeStruct((n,) + block...  62.1 us
    ppermute x3, waiting for transfers between devices, shards(): half_there = lax.ppermute(half, 'col', [(0, 1), (1, 0)])  5.48 us
    ppermute x3, starting transfers between devices, shards(): half_there = lax.ppermute(half, 'col', [(0, 1), (1, 0)])  5 us
  transfers between devices with their start and end apart: 3, of which 2 were waited for; matrix products, arithmetic and copies ran while one was open for 5% of the time, Pallas kernels for 25%

profile of v4, /device:TPU:0, one launch (start us, length us, event | category | flops | bytes accessed | tf_op | source)
XLA Modules:
  0.0 203.7 jit_solution(15139209289580687789)
XLA Ops:
  0.0 0.1 pad.8.clone
  0.1 0.8 copy.7
  0.8 1.4 add_add_fusion.meta_ref
  2.2 0.0 copy-start
  2.2 114.0 %gather.1 = (bf16[8,16,5,128,128]{4,3,2,1,0:T(8,128)(2,1)}, s32[8,16,128]{2,1,0:T(8,128)}, bf16[8,5,128,128]{3,2,1,0:T(8,128)(2,1)}, s32[16,128]{1,0:T(8,128)}) custom-call(bf16[16,5,128,128]{3,2,1,0:T(8,128)(2,1)} %here.5, s32[16,128]{1,0:T(8,128)} %add_add_fusion.meta_ref), custom_call_target="tpu_custom_call" | custom-call | tf_op jit(solution)/shard_map/gather/pallas_call | solution.py:229
  116.3 0.0 copy-done
  116.3 0.7 constant_dynamic-slice_fusion
  117.0 0.0 copy-start.2
  117.0 0.0 copy-start.1
  117.0 0.6 fusion.1
  117.6 0.0 copy-done.2
  117.6 0.5 fusion.2
  118.1 1.6 reshape.37.cols
  119.8 0.6 reshape.44.keep.left_cols
  120.3 0.0 copy-done.1
  120.4 0.6 fusion.3
  120.9 0.1 pad_add_fusion.2
  121.0 0.6 reshape.43.left_cols
  121.6 6.3 %square_0.1 = (f32[24,128,128]{2,1,0:T(8,128)}, bf16[24,128,128]{2,1,0:T(8,128)(2,1)}) custom-call(s32[20]{0:T(128)} %reshape.43.left_cols, s32[640]{0:T(1024)} %reshape.37.cols, s32[24]{0:T(128)} %reshape.44.keep.left_cols, bf16[16,5,128,128]{3,2,1,0:T(8,128)(2,1)} %here.5, bf16[8,5,128,128]{3,2,1,0:T(8,128)(2,1)} %get-tuple-element.17.there, ...), custom_call_target="tpu_custom_call" | custom-call | flops 1000 | bytes 1000 | tf_op jit(solution)/shard_map/square_0/pallas_call | solution.py:452
  127.9 1.6 collective-permute-start
  129.5 0.8 slice.64
  130.3 0.7 slice.62
  131.0 0.7 slice.63
  131.7 0.6 reshape.42.keep.left_cols
  132.3 0.1 pad_add_fusion
  132.4 0.6 reshape.41.left_cols
  133.0 9.5 %square_2.1 = (f32[48,128,128]{2,1,0:T(8,128)}, bf16[48,128,128]{2,1,0:T(8,128)(2,1)}) custom-call(s32[40]{0:T(128)} %reshape.41.left_cols, s32[640]{0:T(1024)} %reshape.37.cols, s32[48]{0:T(128)} %reshape.42.keep.left_cols, bf16[16,5,128,128]{3,2,1,0:T(8,128)(2,1)} %here.5, bf16[8,5,128,128]{3,2,1,0:T(8,128)(2,1)} %get-tuple-element.17.there, ...), custom_call_target="tpu_custom_call" | custom-call | flops 1000 | bytes 1000 | tf_op jit(solution)/shard_map/square_2/pallas_call | solution.py:452
  142.5 1.2 collective-permute-start.2
  143.7 1.2 reshape.38.keep.left_cols
  145.0 0.8 pad_add_fusion.1
  145.7 0.6 reshape.39.left_cols
  146.3 2.4 %collective-permute-done.rest_1_.blocks = bf16[24,128,128]{2,1,0:T(8,128)(2,1)} collective-permute-done((bf16[24,128,128]{2,1,0:T(8,128)(2,1)}, bf16[24,128,128]{2,1,0:T(8,128)(2,1)}, u32[]{:S(2)}, u32[]{:S(2)}) %collective-permute-start) | collective-permute-done | bytes 786464 | tf_op jit(solution)/shard_map/ppermute | solution.py:528
  148.7 6.2 %square_6.1 = (f32[24,128,128]{2,1,0:T(8,128)}, bf16[24,128,128]{2,1,0:T(8,128)(2,1)}) custom-call(s32[20]{0:T(128)} %reshape.39.left_cols, s32[640]{0:T(1024)} %reshape.37.cols, s32[24]{0:T(128)} %reshape.38.keep.left_cols, bf16[16,5,128,128]{3,2,1,0:T(8,128)(2,1)} %here.5, bf16[8,5,128,128]{3,2,1,0:T(8,128)(2,1)} %get-tuple-element.17.there, ...), custom_call_target="tpu_custom_call" | custom-call | flops 1000 | bytes 1000 | tf_op jit(solution)/shard_map/square_6/pallas_call | solution.py:452
  154.9 2.2 %collective-permute-start.1 = (bf16[24,128,128]{2,1,0:T(8,128)(2,1)}, bf16[24,128,128]{2,1,0:T(8,128)(2,1)}, u32[]{:S(2)}, u32[]{:S(2)}) collective-permute-start(bf16[24,128,128]{2,1,0:T(8,128)(2,1)} %get-tuple-element.22.blocks), channel_id=1, source_target_pairs={{0,2},{2,0},{1,3},{3,1},{4,6},{6,4},{5,7},{7,5},{8,10},{10,8},{9,1... | collective-permute-start | bytes 2359304 | tf_op jit(solution)/shard_map/ppermute | solution.py:528
  157.0 6.8 %cube_here_0.1.base = f32[24,128,128]{2,1,0:T(8,128)} custom-call(s32[24]{0:T(128)} %reshape.44.keep.left_cols, s32[640]{0:T(1024)} %reshape.37.cols, s32[24]{0:T(128)} %reshape.44.keep.left_cols, bf16[24,128,128]{2,1,0:T(8,128)(2,1)} %get-tuple-element.21.blocks, bf16[640,128,128]{2,1,0:T(8,128)(2,1)} %bitcast.6, f32[24,128,128]{2,1,0:T(8,128)} %get-tuple-element.19.rest_0_.base), custom_call_target="tpu_custom_call" | custom-call | flops 1000 | bytes 1000 | tf_op jit(solution)/shard_map/cube_here_0/pallas_call | solution.py:452
  163.9 9.7 %cube_here_2.1.base = f32[48,128,128]{2,1,0:T(8,128)} custom-call(s32[48]{0:T(128)} %reshape.42.keep.left_cols, s32[640]{0:T(1024)} %reshape.37.cols, s32[48]{0:T(128)} %reshape.42.keep.left_cols, bf16[48,128,128]{2,1,0:T(8,128)(2,1)} %get-tuple-element.24.blocks, bf16[640,128,128]{2,1,0:T(8,128)(2,1)} %bitcast.7, f32[48,128,128]{2,1,0:T(8,128)} %get-tuple-element.20.rest_0_.base), custom_call_target="tpu_custom_call" | custom-call | flops 1000 | bytes 1000 | tf_op jit(solution)/shard_map/cube_here_2/pallas_call | solution.py:452
  173.6 0.7 slice.68
  174.3 0.6 reshape.45.left_cols
  174.9 0.8 fusion
  175.7 0.6 reshape.46.left_cols
  176.3 0.6 reshape.36.left_cols
  176.9 6.1 %cube_here_6.1.base = f32[24,128,128]{2,1,0:T(8,128)} custom-call(s32[24]{0:T(128)} %reshape.38.keep.left_cols, s32[640]{0:T(1024)} %reshape.37.cols, s32[24]{0:T(128)} %reshape.38.keep.left_cols, bf16[24,128,128]{2,1,0:T(8,128)(2,1)} %get-tuple-element.22.blocks, bf16[640,128,128]{2,1,0:T(8,128)(2,1)} %bitcast.8, f32[24,128,128]{2,1,0:T(8,128)} %get-tuple-element.23.base), custom_call_target="tpu_custom_call" | custom-call | flops 1000 | bytes 1000 | tf_op jit(solution)/shard_map/cube_here_6/pallas_call | solution.py:452
  183.1 5.2 %cube_there_0.1.rest_0_ = bf16[96,128,128]{2,1,0:T(8,128)(2,1)} custom-call(s32[24]{0:T(128)} %reshape.46.left_cols, s32[640]{0:T(1024)} %reshape.37.cols, s32[24]{0:T(128)} %reshape.44.keep.left_cols, bf16[24,128,128]{2,1,0:T(8,128)(2,1)} %collective-permute-done.rest_1_.blocks, bf16[640,128,128]{2,1,0:T(8,128)(2,1)} %bitcast.9, ...), custom_call_target="tpu_custom_call" | custom-call | flops 1000 | bytes 1000 | tf_op jit(solution)/shard_map/cube_there_0/pallas_call | solution.py:452
  188.2 0.0 collective-permute-done.2.blocks
  188.2 7.1 %cube_there_2.1.rest_0_ = bf16[96,128,128]{2,1,0:T(8,128)(2,1)} custom-call(s32[48]{0:T(128)} %reshape.45.left_cols, s32[640]{0:T(1024)} %reshape.37.cols, s32[48]{0:T(128)} %reshape.42.keep.left_cols, bf16[48,128,128]{2,1,0:T(8,128)(2,1)} %collective-permute-done.2.blocks, bf16[640,128,128]{2,1,0:T(8,128)(2,1)} %bitcast.10, ...), custom_call_target="tpu_custom_call", output_to_operand_aliasing={{}: (6, {})} | custom-call | flops 1000 | bytes 1000 | tf_op jit(solution)/shard_map/cube_there_2/pallas_call | solution.py:452
  195.4 3.1 %collective-permute-done.1.blocks = bf16[24,128,128]{2,1,0:T(8,128)(2,1)} collective-permute-done((bf16[24,128,128]{2,1,0:T(8,128)(2,1)}, bf16[24,128,128]{2,1,0:T(8,128)(2,1)}, u32[]{:S(2)}, u32[]{:S(2)}) %collective-permute-start.1) | collective-permute-done | bytes 786464 | tf_op jit(solution)/shard_map/ppermute | solution.py:528
  198.5 5.2 %cube_there_6.1 = bf16[96,128,128]{2,1,0:T(8,128)(2,1)} custom-call(s32[24]{0:T(128)} %reshape.36.left_cols, s32[640]{0:T(1024)} %reshape.37.cols, s32[24]{0:T(128)} %reshape.38.keep.left_cols, bf16[24,128,128]{2,1,0:T(8,128)(2,1)} %collective-permute-done.1.blocks, bf16[640,128,128]{2,1,0:T(8,128)(2,1)} %bitcast.11, ...), custom_call_target="tpu_custom_call", output_to_operand_aliasing={{}: (6, {})} | custom-call | flops 1000 | bytes 1000 | tf_op jit(solution)/shard_map/cube_there_6/pallas_call | solution.py:452
  (1 shorter events, 0.0 us)
Async XLA Ops:
  2.2 114.1 %copy-start = (s32[16,128]{1,0:T(8,128)S(1)}, s32[16,128]{1,0:T(8,128)}, u32[]{:S(2)}) copy-start(s32[16,128]{1,0:T(8,128)} %add_add_fusion.meta_ref) | copy-start | bytes 24580
  117.0 0.6 copy-start.2
  117.0 3.4 %copy-start.1 = (s32[8,128]{1,0:T(8,128)}, s32[8,128]{1,0:T(8,128)S(1)}, u32[]{:S(2)}) copy-start(s32[8,128]{1,0:T(8,128)S(1)} %get-tuple-element.34) | copy-start | bytes 12292
  127.9 20.8 %collective-permute-start = (bf16[24,128,128]{2,1,0:T(8,128)(2,1)}, bf16[24,128,128]{2,1,0:T(8,128)(2,1)}, u32[]{:S(2)}, u32[]{:S(2)}) collective-permute-start(bf16[24,128,128]{2,1,0:T(8,128)(2,1)} %get-tuple-element.21.blocks), channel_id=1, source_target_pairs={{0,2},{2,0},{1,3},{3,1},{4,6},{6,4},{5,7},{7,5},{8,10},{10,8},{9,1... | collective-permute-start | bytes 2359304 | tf_op jit(solution)/shard_map/ppermute | solution.py:528
  142.5 45.7 %collective-permute-start.2 = (bf16[48,128,128]{2,1,0:T(8,128)(2,1)}, bf16[48,128,128]{2,1,0:T(8,128)(2,1)}, u32[]{:S(2)}, u32[]{:S(2)}) collective-permute-start(bf16[48,128,128]{2,1,0:T(8,128)(2,1)} %get-tuple-element.24.blocks), channel_id=1, source_target_pairs={{0,2},{2,0},{1,3},{3,1},{4,6},{6,4},{5,7},{7,5},{8,10},{10,8},{9,1... | collective-permute-start | bytes 4718600 | tf_op jit(solution)/shard_map/ppermute | solution.py:528
  154.9 43.6 %collective-permute-start.1 = (bf16[24,128,128]{2,1,0:T(8,128)(2,1)}, bf16[24,128,128]{2,1,0:T(8,128)(2,1)}, u32[]{:S(2)}, u32[]{:S(2)}) collective-permute-start(bf16[24,128,128]{2,1,0:T(8,128)(2,1)} %get-tuple-element.22.blocks), channel_id=1, source_target_pairs={{0,2},{2,0},{1,3},{3,1},{4,6},{6,4},{5,7},{7,5},{8,10},{10,8},{9,1... | collective-permute-start | bytes 2359304 | tf_op jit(solution)/shard_map/ppermute | solution.py:528
